TPU v7x, 512 devices: a whole 4x4x16 slice. The times are simulated.
512 devices in a mesh: ctx: 16 (over y, x), exp: 32 (over z, core).
Axes of the slice: x: 4, y: 4, z: 16, core: 2. Of those that a mesh axis runs over, the one named last changes fastest.
Arguments:
- query_heads: bfloat16 [16384, 32, 128], P('ctx', 'exp'), may hold values from -0.59765625 to 0.59765625
- key_heads: bfloat16 [16384, 32, 128], P('ctx', 'exp'), may hold values from -0.59765625 to 0.59765625
- value_heads: bfloat16 [16384, 32, 128], P('ctx', 'exp'), may hold values from -6 to 6
- out_grad: bfloat16 [16384, 32, 128], P('ctx', 'exp'), may hold values from -0.29882812 to 0.29882812
- log_decay: bfloat16 [16384, 32, 128], P('ctx', 'exp'), may hold values from -1 to 0, as said below
- start_state: float32 [16, 32, 128, 128], P('ctx', 'exp'), may hold values from -24 to 24
- layer_grad: bfloat16 [16384, 2304], P(('ctx', 'exp')), may hold values from -6 to 6
- gate_weights: float32 [16384, 8], P(('ctx', 'exp')), may hold values from 0.1 to 1
- routes: int32 [16384, 8], P(('ctx', 'exp')), may hold values from 0 to 31, all different within a row; in each aligned block of 32 rows (0 to 31, 32 to 63, ...) at most 16 rows name the same one
- expert_down: bfloat16 [32, 512, 2304], P('exp'), may hold values from -0.125 to 0.125
Outputs:
- query_grad: bfloat16 [16384, 32, 128], P('ctx', 'exp')
- key_grad: bfloat16 [16384, 32, 128], P('ctx', 'exp')
- value_grad: bfloat16 [16384, 32, 128], P('ctx', 'exp')
- hidden_grad: bfloat16 [16, 32, 32, 16, 512], P('ctx', None, 'exp')
Inputs may be any that keep to these rules, and one draw needn't show every extreme that they name: `routes`: each row names 8 different experts. Within the 32 rows of one device no expert is named by more than 16 rows, a bound that some block reaches. `log_decay`: every entry is at most zero.
All inputs are finite; a program needn't handle non-finite values.
Results may differ from a plain program's by a relative error of at most 0.0049.
Values may be sent and summed in bfloat16 or wider, within the bound.
No kernel may reach another device: no remote copies, remote signals or barrier semaphores. Data moves between devices by JAX's collectives and lax.ppermute only.
A program may use at most 64 MiB of HBM per device.

v0:
```python
import jax
import jax.numpy as jnp
from jax import lax
from jax.sharding import PartitionSpec as P

EXPERTS = 32
MOST = 16


BEST_MATMUL_MODE = lax.Precision.HIGHEST


def shifted(shard, axis, by):
    peers = lax.axis_size(axis)
    pairs = [(i, i + by) for i in range(peers) if 0 <= i + by < peers]
    return lax.ppermute(shard, axis, pairs)


def contraction_dimension_pairs(form, left, right):
    return jnp.einsum(
        form, left, right, precision=BEST_MATMUL_MODE, preferred_element_type=jnp.float32
    )


def advance(running_state, item):
    factor, addition = item
    return (factor[:, None] * running_state + addition, running_state)


def retreat(carried, item):
    factor, addition = item
    return (addition + factor[:, None] * carried, carried)


def local(
    query_heads,
    key_heads,
    value_heads,
    out_grad,
    log_decay,
    start_state,
    layer_grad,
    gate_weights,
    routes,
    expert_down,
):
    length = query_heads.shape[0]
    width = min(64, length)
    count = length // width
    queries = query_heads[:, 0, :].astype(jnp.float32).reshape(count, width, -1)
    key_rows = key_heads[:, 0, :].astype(jnp.float32).reshape(count, width, -1)
    value_row_list = value_heads[:, 0, :].astype(jnp.float32).reshape(count, width, -1)
    gradient_rows = out_grad[:, 0, :].astype(jnp.float32).reshape(count, width, -1)
    decays = log_decay[:, 0, :].astype(jnp.float32).reshape(count, width, -1)
    places = lax.iota(jnp.int32, width)
    lower = (places[:, None] >= places[None, :]).astype(jnp.float32)
    cumulative = contraction_dimension_pairs("ts,nsk->ntk", lower, decays)
    block_ends = cumulative[:, -1, :]
    enlarged = queries * jnp.exp(cumulative)
    reduced = key_rows * jnp.exp(-cumulative)
    tail_scale = jnp.exp(block_ends[:, None, :] - cumulative)
    trailing_key_rows = key_rows * tail_scale
    local_summands = contraction_dimension_pairs("loc,loh->lch", enlarged, gradient_rows)
    offsets = jnp.cumsum(block_ends, axis=0) - block_ends
    message = jnp.sum(jnp.exp(offsets)[:, :, None] * local_summands, axis=0)
    whole_decay = jnp.exp(jnp.sum(block_ends, axis=0))
    end_factor = jnp.exp(block_ends)
    partial_terms = contraction_dimension_pairs("ldr,ldo->lro", trailing_key_rows, value_row_list)
    unused_state, start_times = lax.scan(advance, start_state[0, 0], (end_factor, partial_terms))

    def relay(number, received):
        outgoing = message + whole_decay[:, None] * received
        return shifted(outgoing, "ctx", -1)

    incoming = lax.fori_loop(0, lax.axis_size("ctx") - 1, relay, jnp.zeros_like(message))
    unused_carry, arrival_times = lax.scan(
        retreat, incoming, (end_factor, local_summands), reverse=True
    )
    score_matrix = (
        contraction_dimension_pairs("ntv,nsv->nts", gradient_rows, value_row_list) * lower
    )
    affinity = contraction_dimension_pairs("nuk,ntk->nut", enlarged, reduced) * lower
    query_grad = jnp.exp(cumulative) * (
        contraction_dimension_pairs("ruo,rho->ruh", gradient_rows, start_times)
        + contraction_dimension_pairs("agc,acw->agw", score_matrix, reduced)
    )
    key_grad = jnp.exp(-cumulative) * contraction_dimension_pairs(
        "nst,nsk->ntk", score_matrix, enlarged
    ) + tail_scale * contraction_dimension_pairs("ruo,rho->ruh", value_row_list, arrival_times)
    value_grad = contraction_dimension_pairs(
        "nut,nuv->ntv", affinity, gradient_rows
    ) + contraction_dimension_pairs("jox,jxa->joa", trailing_key_rows, arrival_times)
    model_width = layer_grad.shape[1]
    local_count = expert_down.shape[0]
    flat_routes = routes.reshape(-1)
    indicator_matrix = (flat_routes[:, None] == lax.iota(jnp.int32, EXPERTS)[None, :]).astype(
        jnp.int32
    )
    before = jnp.cumsum(indicator_matrix, axis=0) - indicator_matrix
    position = flat_routes * MOST + jnp.sum(before * indicator_matrix, axis=1)
    scaled = (
        (gate_weights[:, :, None] * layer_grad[:, None, :].astype(jnp.float32))
        .astype(jnp.bfloat16)
        .reshape(-1, model_width)
    )
    buffer = (
        jnp.zeros((EXPERTS * MOST, model_width), jnp.bfloat16)
        .at[position]
        .set(scaled)
        .reshape(EXPERTS, MOST, model_width)
    )
    received = lax.all_to_all(buffer, "exp", split_axis=0, concat_axis=0, tiled=True)
    senders = received.shape[0] // local_count
    shaped = received.reshape(senders, local_count, received.shape[1], received.shape[2])
    product = jnp.einsum(
        "slmd,lfd->slmf", shaped, expert_down, preferred_element_type=jnp.float32
    ).astype(jnp.bfloat16)
    hidden = product.reshape(senders * local_count, received.shape[1], product.shape[3])
    hidden_grad = hidden.reshape(
        1, hidden.shape[0] // local_count, local_count, hidden.shape[1], hidden.shape[2]
    )
    return (
        query_grad.reshape(length, 1, -1).astype(jnp.bfloat16),
        key_grad.reshape(length, 1, -1).astype(jnp.bfloat16),
        value_grad.reshape(length, 1, -1).astype(jnp.bfloat16),
        hidden_grad,
    )


def solution(mesh):
    return jax.shard_map(
        local,
        mesh=mesh,
        in_specs=(
            P("ctx", "exp", None),
            P("ctx", "exp", None),
            P("ctx", "exp", None),
            P("ctx", "exp", None),
            P("ctx", "exp", None),
            P("ctx", "exp", None, None),
            P(("ctx", "exp"), None),
            P(("ctx", "exp"), None),
            P(("ctx", "exp"), None),
            P("exp", None, None),
        ),
        out_specs=(
            P("ctx", "exp", None),
            P("ctx", "exp", None),
            P("ctx", "exp", None),
            P("ctx", None, "exp", None, None),
        ),
        check_vma=False,
    )
```

profile of v0, /device:TPU:6, one launch (start us, length us, event | category | flops | bytes accessed | tf_op | source)
XLA Modules:
  0.0 252.1 jit_solution(12575464614881623915)
XLA Ops:
  5.3 4.1 %scatter_custom_fusion = bf16[512,2304]{1,0:T(8,128)(2,1)} fusion(s32[256]{0:T(256)S(1)} %bitcast.137, f32[32,2304]{1,0:T(8,128)S(1)} %convert_element_type.108, f32[256]{0:T(256)S(1)} %mul.140, bf16[]{:T(256)} %constant.68.clone.1), kind=kCustom, calls=%fused_computation.30 | custom fusion | flops 1179648 | bytes 2655234 | tf_op jit(solution)/shard_map/scatter | solution.py:109
  9.4 15.9 %all-to-all-start = ((bf16[32,16,2304]{2,1,0:T(8,128)(2,1)}), bf16[32,16,2304]{2,1,0:T(8,128)(2,1)}, u32[]{:S(2)}, u32[]{:S(2)}) async-start(bf16[32,16,2304]{2,1,0:T(8,128)(2,1)} %bitcast.111), calls=%async_computation | async-start | bytes 4718592 | tf_op jit(solution)/shard_map/all_to_all | solution.py:112
  27.2 3.0 %fusion.22 = f32[16,128,128]{2,1,0:T(8,128)} fusion(bf16[16,64,128]{2,1,0:T(8,128)(2,1)} %bitcast.124, bf16[16,64,128]{2,1,0:T(8,128)(2,1)S(1)} %bitcast.118, f32[16,64,128]{2,1,0:T(8,128)S(1)} %convolution_bitcast_fusion.2, f32[16,128]{1,0:T(8,128)S(1)} %bitcast.129), kind=kOutput, calls=%fused_computation.40 | convolution fusion | flops 201719808 | bytes 2105344 | tf_op jit(solution)/shard_map/ldr,ldo->lro/dot_general | solution.py:20
  38.9 36.1 %while.38 = (s32[]{:T(128)}, f32[128,128]{1,0:T(8,128)S(1)}, f32[16,128,128]{2,1,0:T(8,128)}, f32[16,128]{1,0:T(8,128)}, f32[16,128,128]{2,1,0:T(8,128)}, /*index=5*/s32[]{:T(128)}) while((s32[]{:T(128)}, f32[128,128]{1,0:T(8,128)S(1)}, f32[16,128,128]{2,1,0:T(8,128)}, f32[16,128]{1,0:T(8,128)}, f32[16,128,128]{2,1,0:T(8,128)}, ...), condition=%wide.region_1.2_spmd, body=%wide.region_0.0_spmd.sunk | while | flops 32770 | bytes 329805 | solution.py:69
  79.9 125.8 %while.39 = (s32[]{:T(128)}, f32[128,128]{1,0:T(8,128)S(1)}, f32[128]{0:T(128)S(1)}, f32[128,128]{1,0:T(8,128)S(1)}, s32[]{:T(128)}) while((s32[]{:T(128)}, f32[128,128]{1,0:T(8,128)S(1)}, f32[128]{0:T(128)S(1)}, f32[128,128]{1,0:T(8,128)S(1)}, s32[]{:T(128)}) %tuple.72), condition=%wide.region_6.7_spmd, body=%wide.region_5.6_spmd.sunk | while | flops 32770 | bytes 459365 | solution.py:75
  80.0 2.7 %collective-permute-start = (f32[128,128]{1,0:T(8,128)S(1)}, f32[128,128]{1,0:T(8,128)S(1)}, u32[]{:S(2)}, u32[]{:S(2)}) collective-permute-start(f32[128,128]{1,0:T(8,128)S(1)} %multiply_add_fusion.2), channel_id=1, source_target_pairs={{32,0},{64,32},{96,64},{128,96},{160,128},{192,160},{224,192},{256... | collective-permute-start | bytes 196616 | tf_op jit(solution)/shard_map/while/body/eval_jaxpr/ppermute | solution.py:16
  82.7 5.5 %collective-permute-done = f32[128,128]{1,0:T(8,128)S(1)} collective-permute-done((f32[128,128]{1,0:T(8,128)S(1)}, f32[128,128]{1,0:T(8,128)S(1)}, u32[]{:S(2)}, u32[]{:S(2)}) %collective-permute-start) | collective-permute-done | bytes 65568 | tf_op jit(solution)/shard_map/while/body/eval_jaxpr/ppermute | solution.py:16
  90.3 6.3 %collective-permute-done = f32[128,128]{1,0:T(8,128)S(1)} collective-permute-done((f32[128,128]{1,0:T(8,128)S(1)}, f32[128,128]{1,0:T(8,128)S(1)}, u32[]{:S(2)}, u32[]{:S(2)}) %collective-permute-start) | collective-permute-done | bytes 65568 | tf_op jit(solution)/shard_map/while/body/eval_jaxpr/ppermute | solution.py:16
  98.6 6.3 %collective-permute-done = f32[128,128]{1,0:T(8,128)S(1)} collective-permute-done((f32[128,128]{1,0:T(8,128)S(1)}, f32[128,128]{1,0:T(8,128)S(1)}, u32[]{:S(2)}, u32[]{:S(2)}) %collective-permute-start) | collective-permute-done | bytes 65568 | tf_op jit(solution)/shard_map/while/body/eval_jaxpr/ppermute | solution.py:16
  107.0 6.3 %collective-permute-done = f32[128,128]{1,0:T(8,128)S(1)} collective-permute-done((f32[128,128]{1,0:T(8,128)S(1)}, f32[128,128]{1,0:T(8,128)S(1)}, u32[]{:S(2)}, u32[]{:S(2)}) %collective-permute-start) | collective-permute-done | bytes 65568 | tf_op jit(solution)/shard_map/while/body/eval_jaxpr/ppermute | solution.py:16
  115.3 6.3 %collective-permute-done = f32[128,128]{1,0:T(8,128)S(1)} collective-permute-done((f32[128,128]{1,0:T(8,128)S(1)}, f32[128,128]{1,0:T(8,128)S(1)}, u32[]{:S(2)}, u32[]{:S(2)}) %collective-permute-start) | collective-permute-done | bytes 65568 | tf_op jit(solution)/shard_map/while/body/eval_jaxpr/ppermute | solution.py:16
  123.7 6.3 %collective-permute-done = f32[128,128]{1,0:T(8,128)S(1)} collective-permute-done((f32[128,128]{1,0:T(8,128)S(1)}, f32[128,128]{1,0:T(8,128)S(1)}, u32[]{:S(2)}, u32[]{:S(2)}) %collective-permute-start) | collective-permute-done | bytes 65568 | tf_op jit(solution)/shard_map/while/body/eval_jaxpr/ppermute | solution.py:16
  132.1 6.3 %collective-permute-done = f32[128,128]{1,0:T(8,128)S(1)} collective-permute-done((f32[128,128]{1,0:T(8,128)S(1)}, f32[128,128]{1,0:T(8,128)S(1)}, u32[]{:S(2)}, u32[]{:S(2)}) %collective-permute-start) | collective-permute-done | bytes 65568 | tf_op jit(solution)/shard_map/while/body/eval_jaxpr/ppermute | solution.py:16
  140.4 6.8 %collective-permute-done = f32[128,128]{1,0:T(8,128)S(1)} collective-permute-done((f32[128,128]{1,0:T(8,128)S(1)}, f32[128,128]{1,0:T(8,128)S(1)}, u32[]{:S(2)}, u32[]{:S(2)}) %collective-permute-start) | collective-permute-done | bytes 65568 | tf_op jit(solution)/shard_map/while/body/eval_jaxpr/ppermute | solution.py:16
  149.2 6.3 %collective-permute-done = f32[128,128]{1,0:T(8,128)S(1)} collective-permute-done((f32[128,128]{1,0:T(8,128)S(1)}, f32[128,128]{1,0:T(8,128)S(1)}, u32[]{:S(2)}, u32[]{:S(2)}) %collective-permute-start) | collective-permute-done | bytes 65568 | tf_op jit(solution)/shard_map/while/body/eval_jaxpr/ppermute | solution.py:16
  157.6 6.3 %collective-permute-done = f32[128,128]{1,0:T(8,128)S(1)} collective-permute-done((f32[128,128]{1,0:T(8,128)S(1)}, f32[128,128]{1,0:T(8,128)S(1)}, u32[]{:S(2)}, u32[]{:S(2)}) %collective-permute-start) | collective-permute-done | bytes 65568 | tf_op jit(solution)/shard_map/while/body/eval_jaxpr/ppermute | solution.py:16
  166.0 6.3 %collective-permute-done = f32[128,128]{1,0:T(8,128)S(1)} collective-permute-done((f32[128,128]{1,0:T(8,128)S(1)}, f32[128,128]{1,0:T(8,128)S(1)}, u32[]{:S(2)}, u32[]{:S(2)}) %collective-permute-start) | collective-permute-done | bytes 65568 | tf_op jit(solution)/shard_map/while/body/eval_jaxpr/ppermute | solution.py:16
  174.3 6.3 %collective-permute-done = f32[128,128]{1,0:T(8,128)S(1)} collective-permute-done((f32[128,128]{1,0:T(8,128)S(1)}, f32[128,128]{1,0:T(8,128)S(1)}, u32[]{:S(2)}, u32[]{:S(2)}) %collective-permute-start) | collective-permute-done | bytes 65568 | tf_op jit(solution)/shard_map/while/body/eval_jaxpr/ppermute | solution.py:16
  182.7 6.3 %collective-permute-done = f32[128,128]{1,0:T(8,128)S(1)} collective-permute-done((f32[128,128]{1,0:T(8,128)S(1)}, f32[128,128]{1,0:T(8,128)S(1)}, u32[]{:S(2)}, u32[]{:S(2)}) %collective-permute-start) | collective-permute-done | bytes 65568 | tf_op jit(solution)/shard_map/while/body/eval_jaxpr/ppermute | solution.py:16
  191.0 6.3 %collective-permute-done = f32[128,128]{1,0:T(8,128)S(1)} collective-permute-done((f32[128,128]{1,0:T(8,128)S(1)}, f32[128,128]{1,0:T(8,128)S(1)}, u32[]{:S(2)}, u32[]{:S(2)}) %collective-permute-start) | collective-permute-done | bytes 65568 | tf_op jit(solution)/shard_map/while/body/eval_jaxpr/ppermute | solution.py:16
  199.4 6.3 %collective-permute-done = f32[128,128]{1,0:T(8,128)S(1)} collective-permute-done((f32[128,128]{1,0:T(8,128)S(1)}, f32[128,128]{1,0:T(8,128)S(1)}, u32[]{:S(2)}, u32[]{:S(2)}) %collective-permute-start) | collective-permute-done | bytes 65568 | tf_op jit(solution)/shard_map/while/body/eval_jaxpr/ppermute | solution.py:16
  206.8 36.2 %while.40 = (s32[]{:T(128)}, f32[128,128]{1,0:T(8,128)S(1)}, f32[16,128,128]{2,1,0:T(8,128)}, f32[16,128,128]{2,1,0:T(8,128)}, f32[16,128]{1,0:T(8,128)}, /*index=5*/s32[]{:T(128)}, s32[]{:T(128)}) while((s32[]{:T(128)}, f32[128,128]{1,0:T(8,128)S(1)}, f32[16,128,128]{2,1,0:T(8,128)}, f32[16,128,128]{2,1,0:T(8,128)}, f32[16,128]{1,0:T(8,128)}, ...), condition=%wide.region_8.9_spmd, body=%wide.region_7.8_spmd.sunk | while | flops 32771 | bytes 329317 | solution.py:76
  243.0 3.3 %fusion.15 = bf16[16,64,128]{2,1,0:T(8,128)(2,1)} fusion(f32[16,64,128]{2,1,0:T(8,128)} %fusion.33, f32[16,128,128]{2,1,0:T(8,128)} %get-tuple-element.158, bf16[16,64,128]{2,1,0:T(8,128)(2,1)S(1)} %bitcast.120, f32[16,64,128]{2,1,0:T(8,128)S(1)} %convolution_bitcast_fusion.2, f32[16,128]{1,0:T(8,128)S(1)} %bitcast.130), kind=kOutput, calls=%fused_computation.28 | convolution fusion | flops 201981952 | bytes 2629632 | tf_op jit(solution)/shard_map/jox,jxa->joa/dot_general | solution.py:20
  248.2 3.9 %fusion.8 = bf16[1,32,1,16,512]{4,3,2,1,0:T(8,128)(2,1)} fusion(bf16[32,16,2304]{2,1,0:T(8,128)(2,1)} %all-to-all-done, bf16[1,512,2304]{2,1,0:T(8,128)(2,1)S(1)} %copy-done), kind=kOutput, calls=%fused_computation.16 | convolution fusion | flops 1208221696 | bytes 5242880 | tf_op jit(solution)/shard_map/slmd,lfd->slmf/dot_general | solution.py:115
  (181 shorter events, 122.7 us)
Async XLA Ops:
  0.6 247.6 %copy-start = (bf16[1,512,2304]{2,1,0:T(8,128)(2,1)S(1)}, bf16[1,512,2304]{2,1,0:T(8,128)(2,1)}, u32[]{:S(2)}) copy-start(bf16[1,512,2304]{2,1,0:T(8,128)(2,1)} %param.25) | copy-start | bytes 7077892
  9.4 17.8 %copy-start.4 = (bf16[1024,1,128]{2,0,1:T(8,128)(2,1)S(1)}, bf16[1024,1,128]{2,0,1:T(8,128)(2,1)}, u32[]{:S(2)}) copy-start(bf16[1024,1,128]{2,0,1:T(8,128)(2,1)} %param.17) | copy-start | bytes 786436
  9.4 238.8 %all-to-all-start = ((bf16[32,16,2304]{2,1,0:T(8,128)(2,1)}), bf16[32,16,2304]{2,1,0:T(8,128)(2,1)}, u32[]{:S(2)}, u32[]{:S(2)}) async-start(bf16[32,16,2304]{2,1,0:T(8,128)(2,1)} %bitcast.111), calls=%async_computation | async-start | bytes 4718592 | tf_op jit(solution)/shard_map/all_to_all | solution.py:112
  25.3 4.9 %copy-start.6 = (bf16[1024,1,128]{2,0,1:T(8,128)(2,1)S(1)}, bf16[1024,1,128]{2,0,1:T(8,128)(2,1)}, u32[]{:S(2)}) copy-start(bf16[1024,1,128]{2,0,1:T(8,128)(2,1)} %param.16) | copy-start | bytes 786436
  26.6 4.7 %copy-start.8 = (bf16[1024,1,128]{2,0,1:T(8,128)(2,1)S(1)}, bf16[1024,1,128]{2,0,1:T(8,128)(2,1)}, u32[]{:S(2)}) copy-start(bf16[1024,1,128]{2,0,1:T(8,128)(2,1)} %param.18) | copy-start | bytes 786436
  27.2 5.3 %copy-start.3 = (bf16[1024,1,128]{2,0,1:T(8,128)(2,1)S(1)}, bf16[1024,1,128]{2,0,1:T(8,128)(2,1)}, u32[]{:S(2)}) copy-start(bf16[1024,1,128]{2,0,1:T(8,128)(2,1)} %param.19) | copy-start | bytes 786436
  27.2 5.3 %copy-start.7 = (bf16[1024,1,128]{2,0,1:T(8,128)(2,1)S(1)}, bf16[1024,1,128]{2,0,1:T(8,128)(2,1)}, u32[]{:S(2)}) copy-start(bf16[1024,1,128]{2,0,1:T(8,128)(2,1)} %param.16) | copy-start | bytes 786436
  79.9 163.1 %copy-start.5 = (bf16[1024,1,128]{2,0,1:T(8,128)(2,1)S(1)}, bf16[1024,1,128]{2,0,1:T(8,128)(2,1)}, u32[]{:S(2)}) copy-start(bf16[1024,1,128]{2,0,1:T(8,128)(2,1)} %param.17) | copy-start | bytes 786436
  80.0 8.3 %collective-permute-start = (f32[128,128]{1,0:T(8,128)S(1)}, f32[128,128]{1,0:T(8,128)S(1)}, u32[]{:S(2)}, u32[]{:S(2)}) collective-permute-start(f32[128,128]{1,0:T(8,128)S(1)} %multiply_add_fusion.2), channel_id=1, source_target_pairs={{32,0},{64,32},{96,64},{128,96},{160,128},{192,160},{224,192},{256... | collective-permute-start | bytes 196616 | tf_op jit(solution)/shard_map/while/body/eval_jaxpr/ppermute | solution.py:16
  88.3 8.3 %collective-permute-start = (f32[128,128]{1,0:T(8,128)S(1)}, f32[128,128]{1,0:T(8,128)S(1)}, u32[]{:S(2)}, u32[]{:S(2)}) collective-permute-start(f32[128,128]{1,0:T(8,128)S(1)} %multiply_add_fusion.2), channel_id=1, source_target_pairs={{32,0},{64,32},{96,64},{128,96},{160,128},{192,160},{224,192},{256... | collective-permute-start | bytes 196616 | tf_op jit(solution)/shard_map/while/body/eval_jaxpr/ppermute | solution.py:16
  96.7 8.3 %collective-permute-start = (f32[128,128]{1,0:T(8,128)S(1)}, f32[128,128]{1,0:T(8,128)S(1)}, u32[]{:S(2)}, u32[]{:S(2)}) collective-permute-start(f32[128,128]{1,0:T(8,128)S(1)} %multiply_add_fusion.2), channel_id=1, source_target_pairs={{32,0},{64,32},{96,64},{128,96},{160,128},{192,160},{224,192},{256... | collective-permute-start | bytes 196616 | tf_op jit(solution)/shard_map/while/body/eval_jaxpr/ppermute | solution.py:16
  105.1 8.3 %collective-permute-start = (f32[128,128]{1,0:T(8,128)S(1)}, f32[128,128]{1,0:T(8,128)S(1)}, u32[]{:S(2)}, u32[]{:S(2)}) collective-permute-start(f32[128,128]{1,0:T(8,128)S(1)} %multiply_add_fusion.2), channel_id=1, source_target_pairs={{32,0},{64,32},{96,64},{128,96},{160,128},{192,160},{224,192},{256... | collective-permute-start | bytes 196616 | tf_op jit(solution)/shard_map/while/body/eval_jaxpr/ppermute | solution.py:16
  113.4 8.3 %collective-permute-start = (f32[128,128]{1,0:T(8,128)S(1)}, f32[128,128]{1,0:T(8,128)S(1)}, u32[]{:S(2)}, u32[]{:S(2)}) collective-permute-start(f32[128,128]{1,0:T(8,128)S(1)} %multiply_add_fusion.2), channel_id=1, source_target_pairs={{32,0},{64,32},{96,64},{128,96},{160,128},{192,160},{224,192},{256... | collective-permute-start | bytes 196616 | tf_op jit(solution)/shard_map/while/body/eval_jaxpr/ppermute | solution.py:16
  121.8 8.3 %collective-permute-start = (f32[128,128]{1,0:T(8,128)S(1)}, f32[128,128]{1,0:T(8,128)S(1)}, u32[]{:S(2)}, u32[]{:S(2)}) collective-permute-start(f32[128,128]{1,0:T(8,128)S(1)} %multiply_add_fusion.2), channel_id=1, source_target_pairs={{32,0},{64,32},{96,64},{128,96},{160,128},{192,160},{224,192},{256... | collective-permute-start | bytes 196616 | tf_op jit(solution)/shard_map/while/body/eval_jaxpr/ppermute | solution.py:16
  130.1 8.3 %collective-permute-start = (f32[128,128]{1,0:T(8,128)S(1)}, f32[128,128]{1,0:T(8,128)S(1)}, u32[]{:S(2)}, u32[]{:S(2)}) collective-permute-start(f32[128,128]{1,0:T(8,128)S(1)} %multiply_add_fusion.2), channel_id=1, source_target_pairs={{32,0},{64,32},{96,64},{128,96},{160,128},{192,160},{224,192},{256... | collective-permute-start | bytes 196616 | tf_op jit(solution)/shard_map/while/body/eval_jaxpr/ppermute | solution.py:16
  138.5 8.7 %collective-permute-start = (f32[128,128]{1,0:T(8,128)S(1)}, f32[128,128]{1,0:T(8,128)S(1)}, u32[]{:S(2)}, u32[]{:S(2)}) collective-permute-start(f32[128,128]{1,0:T(8,128)S(1)} %multiply_add_fusion.2), channel_id=1, source_target_pairs={{32,0},{64,32},{96,64},{128,96},{160,128},{192,160},{224,192},{256... | collective-permute-start | bytes 196616 | tf_op jit(solution)/shard_map/while/body/eval_jaxpr/ppermute | solution.py:16
  147.3 8.3 %collective-permute-start = (f32[128,128]{1,0:T(8,128)S(1)}, f32[128,128]{1,0:T(8,128)S(1)}, u32[]{:S(2)}, u32[]{:S(2)}) collective-permute-start(f32[128,128]{1,0:T(8,128)S(1)} %multiply_add_fusion.2), channel_id=1, source_target_pairs={{32,0},{64,32},{96,64},{128,96},{160,128},{192,160},{224,192},{256... | collective-permute-start | bytes 196616 | tf_op jit(solution)/shard_map/while/body/eval_jaxpr/ppermute | solution.py:16
  155.7 8.3 %collective-permute-start = (f32[128,128]{1,0:T(8,128)S(1)}, f32[128,128]{1,0:T(8,128)S(1)}, u32[]{:S(2)}, u32[]{:S(2)}) collective-permute-start(f32[128,128]{1,0:T(8,128)S(1)} %multiply_add_fusion.2), channel_id=1, source_target_pairs={{32,0},{64,32},{96,64},{128,96},{160,128},{192,160},{224,192},{256... | collective-permute-start | bytes 196616 | tf_op jit(solution)/shard_map/while/body/eval_jaxpr/ppermute | solution.py:16
  164.0 8.3 %collective-permute-start = (f32[128,128]{1,0:T(8,128)S(1)}, f32[128,128]{1,0:T(8,128)S(1)}, u32[]{:S(2)}, u32[]{:S(2)}) collective-permute-start(f32[128,128]{1,0:T(8,128)S(1)} %multiply_add_fusion.2), channel_id=1, source_target_pairs={{32,0},{64,32},{96,64},{128,96},{160,128},{192,160},{224,192},{256... | collective-permute-start | bytes 196616 | tf_op jit(solution)/shard_map/while/body/eval_jaxpr/ppermute | solution.py:16
  172.4 8.3 %collective-permute-start = (f32[128,128]{1,0:T(8,128)S(1)}, f32[128,128]{1,0:T(8,128)S(1)}, u32[]{:S(2)}, u32[]{:S(2)}) collective-permute-start(f32[128,128]{1,0:T(8,128)S(1)} %multiply_add_fusion.2), channel_id=1, source_target_pairs={{32,0},{64,32},{96,64},{128,96},{160,128},{192,160},{224,192},{256... | collective-permute-start | bytes 196616 | tf_op jit(solution)/shard_map/while/body/eval_jaxpr/ppermute | solution.py:16
  180.7 8.3 %collective-permute-start = (f32[128,128]{1,0:T(8,128)S(1)}, f32[128,128]{1,0:T(8,128)S(1)}, u32[]{:S(2)}, u32[]{:S(2)}) collective-permute-start(f32[128,128]{1,0:T(8,128)S(1)} %multiply_add_fusion.2), channel_id=1, source_target_pairs={{32,0},{64,32},{96,64},{128,96},{160,128},{192,160},{224,192},{256... | collective-permute-start | bytes 196616 | tf_op jit(solution)/shard_map/while/body/eval_jaxpr/ppermute | solution.py:16
  189.1 8.3 %collective-permute-start = (f32[128,128]{1,0:T(8,128)S(1)}, f32[128,128]{1,0:T(8,128)S(1)}, u32[]{:S(2)}, u32[]{:S(2)}) collective-permute-start(f32[128,128]{1,0:T(8,128)S(1)} %multiply_add_fusion.2), channel_id=1, source_target_pairs={{32,0},{64,32},{96,64},{128,96},{160,128},{192,160},{224,192},{256... | collective-permute-start | bytes 196616 | tf_op jit(solution)/shard_map/while/body/eval_jaxpr/ppermute | solution.py:16
  197.4 8.3 %collective-permute-start = (f32[128,128]{1,0:T(8,128)S(1)}, f32[128,128]{1,0:T(8,128)S(1)}, u32[]{:S(2)}, u32[]{:S(2)}) collective-permute-start(f32[128,128]{1,0:T(8,128)S(1)} %multiply_add_fusion.2), channel_id=1, source_target_pairs={{32,0},{64,32},{96,64},{128,96},{160,128},{192,160},{224,192},{256... | collective-permute-start | bytes 196616 | tf_op jit(solution)/shard_map/while/body/eval_jaxpr/ppermute | solution.py:16
  206.8 39.5 %copy-start.9 = (bf16[1024,1,128]{2,0,1:T(8,128)(2,1)S(1)}, bf16[1024,1,128]{2,0,1:T(8,128)(2,1)}, u32[]{:S(2)}) copy-start(bf16[1024,1,128]{2,0,1:T(8,128)(2,1)} %param.18) | copy-start | bytes 786436
  (3 other events, 10.9 us)
where the time goes:
time: 255 us; the launch traced here: 252 us
  waiting for transfers between devices  94.7 us (37%)
  local copies, waits for them, and re-layouts  46.6 us (18%)
  starting transfers between devices  45.5 us (18%)
  other arithmetic  37.8 us (15%)
  matrix products  25.6 us (10%)
    ppermute x15, waiting for transfers between devices, shifted(): return lax.ppermute(shard, axis, pairs)  94.7 us
    ppermute x15, starting transfers between devices, shifted(): return lax.ppermute(shard, axis, pairs)  29.6 us
    dot_general x11, matrix products, contraction_dimension_pairs(): jnp.einsum(form, left, right, precision=BEST_MATMUL_MODE, preferred_eleme...  21.8 us
    dynamic_update_slice x32, local copies, waits for them, and re-layouts, local(): lax.scan(advance, start_state[0, 0], (end_factor, partial_terms))  20 us
    all_to_all x1, starting transfers between devices, local(): lax.all_to_all(buffer, 'exp', split_axis=0, concat_axis=0, tiled=True)  15.9 us
    add x16, other arithmetic, advance(): return (factor[:, None] * running_state + addition, running_state)  14.7 us
    add x16, other arithmetic, retreat(): return (addition + factor[:, None] * carried, carried)  14.7 us
    mul x16, local copies, waits for them, and re-layouts, advance(): return (factor[:, None] * running_state + addition, running_state)  11.1 us
  transfers between devices with their start and end apart: 16, of which 15 were waited for; matrix products, arithmetic and copies ran while one was open for 39% of the time, Pallas kernels for 0%

commit v1 on v0

v1 whole, which is shorter than its diff:
```python
import jax
import jax.numpy as jnp
from jax import lax
from jax.experimental import pallas as pl
from jax.experimental.pallas import tpu as pltpu
from jax.sharding import PartitionSpec as P

EXPERTS = 32
MOST = 16
ROWS = 32
CHUNK = 128
EXTRA = 128
F32 = jnp.float32
BF16 = jnp.bfloat16
NN = (((1,), (0,)), ((), ()))
NT = (((1,), (1,)), ((), ()))
TN = (((0,), (0,)), ((), ()))


def dot(left, right, dims=NN):
    return lax.dot_general(left, right, dims, preferred_element_type=F32)


def call(body, outs, operands, smem=0, hbm=0, scratch=()):
    spaces = [pltpu.SMEM] * smem + [pltpu.HBM] * hbm
    spaces += [pltpu.VMEM] * (len(operands) - len(spaces))
    return pl.pallas_call(
        body,
        out_shape=outs,
        in_specs=[pl.BlockSpec(memory_space=space) for space in spaces],
        out_specs=jax.tree.map(lambda _: pl.BlockSpec(memory_space=pltpu.VMEM), outs),
        scratch_shapes=scratch,
        compiler_params=pltpu.CompilerParams(vmem_limit_bytes=32 * 1024 * 1024),
        cost_estimate=pl.CostEstimate(flops=1000, bytes_accessed=1000, transcendentals=0),
    )(*operands)


def lower_mask():
    rows = lax.broadcasted_iota(jnp.int32, (CHUNK, CHUNK), 0)
    columns = lax.broadcasted_iota(jnp.int32, (CHUNK, CHUNK), 1)
    return rows >= columns


def pack_body(rows_ref, gates_ref, routes_ref, out_ref, gates_here, routes_here, sems):
    width = rows_ref.shape[1]
    copies = [
        pltpu.make_async_copy(gates_ref, gates_here, sems.at[0]),
        pltpu.make_async_copy(routes_ref, routes_here, sems.at[1]),
        pltpu.make_async_copy(rows_ref, out_ref.at[:, pl.ds(0, width)], sems.at[2]),
    ]
    for copy in copies:
        copy.start()
    lanes = lax.broadcasted_iota(jnp.int32, (ROWS, EXTRA), 1)
    dense = jnp.zeros((ROWS, EXTRA), F32)
    copies[0].wait()
    copies[1].wait()
    gates, routes = gates_here[...].T, routes_here[...].T
    for r in range(gates.shape[1]):
        hit = (lanes % EXPERTS) == routes[:, r : r + 1]
        dense = jnp.where(hit, gates[:, r : r + 1], dense)
    high = dense.astype(BF16).astype(F32)
    both = jnp.where(lanes < EXPERTS, high, jnp.where(lanes < 2 * EXPERTS, dense - high, 0.0))
    out_ref[:, width:] = both.astype(BF16)
    copies[2].wait()


def message_body(q_ref, g_ref, d_ref, out_ref):
    lower = lower_mask().astype(BF16)
    total = jnp.zeros((1, q_ref.shape[1]), F32)
    message = jnp.zeros((g_ref.shape[1], q_ref.shape[1]), F32)
    for n in range(q_ref.shape[0] // CHUNK):
        part = pl.ds(n * CHUNK, CHUNK)
        sums = dot(lower, d_ref[part]) + total
        total = sums[CHUNK - 1 :]
        scaled = (q_ref[part].astype(F32) * jnp.exp(sums)).astype(BF16)
        message += dot(g_ref[part], scaled, TN)
    out_ref[: message.shape[0]] = message
    out_ref[message.shape[0] :] = jnp.broadcast_to(jnp.exp(total), (8, total.shape[1]))


def heads_body(
    q_ref, k_ref, v_ref, g_ref, d_ref, start_ref, qg_ref, pk_ref, pv_ref, tail_ref, add_ref
):
    count = q_ref.shape[0] // CHUNK
    keep = lower_mask()
    lower = keep.astype(BF16)
    state = start_ref[...].T
    ends = []
    for n in range(count):
        part = pl.ds(n * CHUNK, CHUNK)
        queries, keys = q_ref[part].astype(F32), k_ref[part].astype(F32)
        values, grads = v_ref[part], g_ref[part]
        sums = dot(lower, d_ref[part])
        end, middle = sums[CHUNK - 1 :], sums[CHUNK // 2 - 1 : CHUNK // 2]
        ends.append(end)
        grow, shrink = jnp.exp(sums - middle), jnp.exp(middle - sums)
        whole = jnp.exp(sums)
        trail = jnp.exp(end - sums)
        enlarged, reduced = (queries * grow).astype(BF16), (keys * shrink).astype(BF16)
        score = jnp.where(keep, dot(grads, values, NT), 0.0).astype(BF16)
        affinity = jnp.where(keep, dot(enlarged, reduced, NT), 0.0).astype(BF16)
        query_grad = whole * dot(grads, state.astype(BF16)) + grow * dot(score, reduced)
        qg_ref[part] = query_grad.astype(BF16)
        pk_ref[part] = shrink * dot(score, enlarged, TN)
        pv_ref[part] = dot(affinity, grads, TN)
        add_ref[n] = dot(grads, (queries * whole).astype(BF16), TN)
        state = state * jnp.exp(end) + dot(values, (keys * trail).astype(BF16), TN)
        tail_ref[part] = end - sums
    later = jnp.zeros_like(ends[0])
    adjoint = jnp.zeros_like(state)
    for n in reversed(range(count)):
        part = pl.ds(n * CHUNK, CHUNK)
        left = tail_ref[part]
        if n < count - 1:
            trail = jnp.exp(left)
            arrived = adjoint.astype(BF16)
            pk_ref[part] += trail * dot(v_ref[part], arrived)
            scaled = (k_ref[part].astype(F32) * trail).astype(BF16)
            pv_ref[part] += dot(scaled, arrived, NT)
        tail_ref[part] = jnp.exp(left + later)
        later = later + ends[n]
        adjoint = add_ref[n] + jnp.exp(ends[n]) * adjoint


def arrival_body(k_ref, v_ref, in_ref, pk_ref, pv_ref, tail_ref, kg_ref, vg_ref):
    arrived = in_ref[: v_ref.shape[1]].astype(BF16)
    tail = tail_ref[...]
    kg_ref[...] = (pk_ref[...] + tail * dot(v_ref[...], arrived)).astype(BF16)
    scaled = (k_ref[...].astype(F32) * tail).astype(BF16)
    vg_ref[...] = (pv_ref[...] + dot(scaled, arrived, NT)).astype(BF16)


def slots(expert, rows_ref, down_ref, store):
    width = down_ref.shape[1]
    hidden = dot(rows_ref[:, :width], down_ref[...], NT)
    blocks = rows_ref.shape[0] // ROWS
    for first in range(0, blocks, 4):
        number = min(4, blocks - first)
        size = number * ROWS
        part = slice(first * ROWS, first * ROWS + size)
        gates = rows_ref[part, width:].astype(F32)
        lanes = lax.broadcasted_iota(jnp.int32, (size, EXTRA), 1)
        row = lax.broadcasted_iota(jnp.int32, (size, EXTRA), 0)
        high = jnp.sum(jnp.where(lanes == expert, gates, 0.0), axis=1, keepdims=True)
        low = jnp.sum(jnp.where(lanes == expert + EXPERTS, gates, 0.0), axis=1, keepdims=True)
        taken = jnp.broadcast_to(high > 0.0, (size, EXTRA))
        square = lax.broadcasted_iota(jnp.int32, (size, size), 0)
        across = lax.broadcasted_iota(jnp.int32, (size, size), 1)
        earlier = ((square > across) & (square // ROWS == across // ROWS)).astype(BF16)
        place = dot(earlier, taken.astype(BF16)).astype(jnp.int32) + (row // ROWS) * MOST
        hit = taken & (place == lanes)
        high = jnp.where(hit, high, 0.0).astype(BF16)
        low = jnp.where(hit, low, 0.0).astype(BF16)
        block = hidden[part]
        upper = block.astype(BF16)
        lower = (block - upper.astype(F32)).astype(BF16)
        result = dot(high, upper, TN) + dot(high, lower, TN) + dot(low, upper, TN)
        result = result.astype(BF16)
        for b in range(number):
            store(first + b, result[b * MOST : (b + 1) * MOST])


def hidden_body(me_ref, rows_ref, down_ref, out_ref):
    def store(block, result):
        out_ref[block * MOST : (block + 1) * MOST] = result

    slots(me_ref[0], rows_ref, down_ref, store)


def sender(me, hops, other, sibling):
    core = (me % 2 + sibling) % 2
    chip = (me // 2 + EXPERTS // 2 + (2 * core - 1) * hops) % (EXPERTS // 2)
    return chip * 2 + (core + other) % 2


def last_body(me_ref, done_ref, mine_ref, theirs_ref, down_ref, out_ref, rows_ref):
    me = me_ref[0]
    here = [(hops, other, 0) for hops in range(1, 5) for other in (0, 1)]
    blocks = [(0, 0, 0), (0, 1, 0), *here, *((h, o, 1) for h, o, _ in here)]
    for i, block in enumerate(blocks):
        out_ref[sender(me, *block)] = done_ref[i * MOST : (i + 1) * MOST]
    here = [*((hops, other, 0) for hops in (5, 6, 7) for other in (0, 1)), (8, 0, 0)]
    blocks = [*here, *((h, o, 1) for h, o, _ in here)]
    half = mine_ref.shape[0]
    rows_ref[:half] = mine_ref[...]
    rows_ref[half:] = theirs_ref[...]

    def store(i, result):
        out_ref[sender(me, *blocks[i])] = result

    slots(me, rows_ref, down_ref, store)


def move(array, hops):
    chips = EXPERTS // 2
    pairs = []
    for chip in range(chips):
        for core in range(2):
            step = hops if core == 0 else -hops
            pairs.append((2 * chip + core, 2 * ((chip + step) % chips) + core))
    return lax.ppermute(array, "exp", pairs)


def swap(array):
    return lax.ppermute(array, "exp", [(i, i ^ 1) for i in range(EXPERTS)])


def from_later(array, by):
    peers = lax.axis_size("ctx")
    return lax.ppermute(array, "ctx", [(i + by, i) for i in range(peers - by)])


def after(array, *others):
    return lax.optimization_barrier((array, *others))[0]


def combine(first, second, states):
    decay = first[states : states + 1]
    own = jnp.where(lax.broadcasted_iota(jnp.int32, first.shape, 0) < states, first, 0.0)
    return own + decay * second


def join_body(*refs):
    *parts, out_ref = refs
    first = 0
    for part in parts:
        out_ref[first : first + part.shape[0]] = part[...]
        first += part.shape[0]


def join(*parts):
    rows = sum(part.shape[0] for part in parts)
    out = jax.ShapeDtypeStruct((rows, parts[0].shape[1]), BF16)
    return call(join_body, out, parts)


def local(
    query_heads,
    key_heads,
    value_heads,
    out_grad,
    log_decay,
    start_state,
    layer_grad,
    gate_weights,
    routes,
    expert_down,
):
    length, _, kd = query_heads.shape
    vd = value_heads.shape[2]
    width = layer_grad.shape[1]
    hidden_width = expert_down.shape[1]
    queries, keys = query_heads.reshape(length, kd), key_heads.reshape(length, kd)
    values, grads = value_heads.reshape(length, vd), out_grad.reshape(length, vd)
    decays = log_decay.reshape(length, kd)
    down = expert_down.reshape(hidden_width, width)
    queries, keys, values, grads, decays, layer_grad, gates, chosen, start = (
        pltpu.with_memory_space_constraint(x, pltpu.HBM)
        for x in (
            queries,
            keys,
            values,
            grads,
            decays,
            layer_grad,
            gate_weights.T,
            routes.T,
            start_state.reshape(kd, vd),
        )
    )
    me = lax.axis_index("exp").astype(jnp.int32).reshape(1)
    struct = jax.ShapeDtypeStruct

    def hidden(array):
        return call(
            hidden_body,
            struct((array.shape[0] // ROWS * MOST, hidden_width), BF16),
            (me, array, down),
            smem=1,
        )

    with jax.named_scope("pack"):
        rows = call(
            pack_body,
            struct((ROWS, width + EXTRA), BF16),
            (layer_grad, gates, chosen),
            hbm=3,
            scratch=(
                pltpu.VMEM(gates.shape, F32),
                pltpu.VMEM(chosen.shape, jnp.int32),
                pltpu.SemaphoreType.DMA((3,)),
            ),
        )
    with jax.named_scope("message"):
        message = call(
            message_body, struct((vd + 8, kd), F32), (queries, grads, decays)
        )
    theirs = after(swap(rows), message)
    both = join(rows, theirs)
    with jax.named_scope("heads"):
        query_grad, key_part, value_part, tail = call(
            heads_body,
            (
                struct((length, kd), BF16),
                struct((length, kd), F32),
                struct((length, vd), F32),
                struct((length, kd), F32),
            ),
            (queries, keys, values, grads, decays, after(start, both)),
            scratch=(pltpu.VMEM((length // CHUNK, vd, kd), F32),),
        )

    rows1, rows2 = move(both, 1), move(both, 2)
    incoming = after(from_later(after(message, both), 1), rows1)
    within = combine(message, incoming, vd)
    rows3 = move(after(rows1, within, key_part), 2)
    rows4 = move(rows2, 2)
    incoming = combine(incoming, after(from_later(within, 2), rows3), vd)
    within = combine(message, incoming, vd)
    rows5 = move(after(rows3, within), 2)
    rows6 = move(rows4, 2)
    incoming = combine(incoming, after(from_later(within, 4), rows5), vd)
    within = combine(message, incoming, vd)
    rows7 = move(rows5, 2)
    with jax.named_scope("experts"):
        early = join(rows1, rows2, rows3, after(rows4, rows5))
        done = hidden(join(both, early, swap(early)))
    rows8 = move(after(rows6, within, done)[:ROWS], 2)
    incoming = combine(incoming, from_later(within, 8), vd)

    with jax.named_scope("arrival"):
        key_grad, value_grad = call(
            arrival_body,
            (struct((length, kd), BF16), struct((length, vd), BF16)),
            (keys, values, incoming, key_part, value_part, tail),
        )

    with jax.named_scope("experts"):
        late = after(join(rows5, rows6, rows7, rows8), incoming)
        hidden_grad = call(
            last_body,
            struct((EXPERTS, MOST, hidden_width), BF16),
            (me, done, late, swap(late), down),
            smem=1,
            scratch=(pltpu.VMEM((2 * late.shape[0], late.shape[1]), BF16),),
        )
    return (
        query_grad.reshape(length, 1, kd),
        key_grad.reshape(length, 1, kd),
        value_grad.reshape(length, 1, vd),
        hidden_grad.reshape(1, EXPERTS, 1, MOST, hidden_width),
    )


def solution(mesh):
    return jax.shard_map(
        local,
        mesh=mesh,
        in_specs=(
            P("ctx", "exp", None),
            P("ctx", "exp", None),
            P("ctx", "exp", None),
            P("ctx", "exp", None),
            P("ctx", "exp", None),
            P("ctx", "exp", None, None),
            P(("ctx", "exp"), None),
            P(("ctx", "exp"), None),
            P(("ctx", "exp"), None),
            P("exp", None, None),
        ),
        out_specs=(
            P("ctx", "exp", None),
            P("ctx", "exp", None),
            P("ctx", "exp", None),
            P("ctx", None, "exp", None, None),
        ),
        check_vma=False,
    )
```

time: 255 us -> 97.5 us (0.38)
  the two profiles are of different devices: /device:TPU:6 before, /device:TPU:29 now
where the time goes in v1:
time: 97.5 us; the launch traced here: 96.8 us
  starting transfers between devices  61 us (63%)
  Pallas kernels  17.1 us (18%)
  waiting for transfers between devices  15 us (15%)
  local copies, waits for them, and re-layouts  2.31 us (2%)
  between operations  1 us (1%)
    ppermute x8, starting transfers between devices, move(): return lax.ppermute(array, 'exp', pairs)  38.5 us
    pallas_call x10, Pallas kernels, call(): pl.pallas_call(body, out_shape=outs, in_specs=[pl.BlockSpec(memory_space=...  17.1 us
    ppermute x8, waiting for transfers between devices, move(): return lax.ppermute(array, 'exp', pairs)  14.8 us
    ppermute x3, starting transfers between devices, swap(): return lax.ppermute(array, 'exp', [(i, i ^ 1) for i in range(EXPERTS)])  11.3 us
    ppermute x4, starting transfers between devices, from_later(): return lax.ppermute(array, 'ctx', [(i + by, i) for i in range(peers - by)])  11.2 us
    unnamed x12, local copies, waits for them, and re-layouts  2.29 us
  transfers between devices with their start and end apart: 15, of which 4 were waited for; matrix products, arithmetic and copies ran while one was open for 0% of the time, Pallas kernels for 12%

profile of v1, /device:TPU:29, one launch (start us, length us, event | category | flops | bytes accessed | tf_op | source)
XLA Modules:
  0.0 96.8 jit_solution(9433105371364850892)
XLA Ops:
  1.6 2.6 %collective-permute-start = (bf16[32,2432]{1,0:T(8,128)(2,1)S(1)}, bf16[32,2432]{1,0:T(8,128)(2,1)S(1)}, u32[]{:S(2)}, u32[]{:S(2)}) collective-permute-start(bf16[32,2432]{1,0:T(8,128)(2,1)S(1)} %pack.1.refs_0_), channel_id=1, source_target_pairs={{0,1},{1,0},{2,3},{3,2},{4,5},{5,4},{6,7},{7,6},{8,9},{9,8},{10,11... | collective-permute-start | bytes 466952 | tf_op jit(solution)/shard_map/ppermute | solution.py:205
  4.2 1.5 %message.1 = f32[136,128]{1,0:T(8,128)S(1)} custom-call(bf16[1024,128]{1,0:T(8,128)(2,1)} %bitcast.30, bf16[1024,128]{1,0:T(8,128)(2,1)} %bitcast.32, bf16[1024,128]{1,0:T(8,128)(2,1)} %bitcast.34), custom_call_target="tpu_custom_call" | custom-call | flops 1000 | bytes 1000 | tf_op jit(solution)/shard_map/message/pallas_call | solution.py:27
  5.8 11.1 %collective-permute-start.2 = (bf16[64,2432]{1,0:T(8,128)(2,1)S(1)}, bf16[64,2432]{1,0:T(8,128)(2,1)S(1)}, u32[]{:S(2)}, u32[]{:S(2)}) collective-permute-start(bf16[64,2432]{1,0:T(8,128)(2,1)S(1)} %shard_map.129.refs_0_), channel_id=1, source_target_pairs={{0,2},{1,31},{2,4},{3,1},{4,6},{5,3},{6,8},{7,5},{8,10},{9,7},{10,... | collective-permute-start | bytes 933896 | tf_op jit(solution)/shard_map/ppermute | solution.py:201
  16.9 2.2 %collective-permute-start.1 = (f32[136,128]{1,0:T(8,128)S(1)}, f32[136,128]{1,0:T(8,128)S(1)}, u32[]{:S(2)}, u32[]{:S(2)}) collective-permute-start(f32[136,128]{1,0:T(8,128)S(1)} %message.1), channel_id=1, source_target_pairs={{32,0},{64,32},{96,64},{128,96},{160,128},{192,160},{224,192},{256... | collective-permute-start | bytes 208904 | tf_op jit(solution)/shard_map/ppermute | solution.py:210
  19.1 3.1 %collective-permute-start.8 = (bf16[64,2432]{1,0:T(8,128)(2,1)S(1)}, bf16[64,2432]{1,0:T(8,128)(2,1)S(1)}, u32[]{:S(2)}, u32[]{:S(2)}) collective-permute-start(bf16[64,2432]{1,0:T(8,128)(2,1)S(1)} %shard_map.129.refs_0_), channel_id=1, source_target_pairs={{0,4},{1,29},{2,6},{3,31},{4,8},{5,1},{6,10},{7,3},{8,12},{9,5},{1... | collective-permute-start | bytes 933896 | tf_op jit(solution)/shard_map/ppermute | solution.py:201
  22.2 4.7 %heads.1 = (bf16[1024,128]{1,0:T(8,128)(2,1)}, f32[1024,128]{1,0:T(8,128)S(1)}, f32[1024,128]{1,0:T(8,128)S(1)}, f32[1024,128]{1,0:T(8,128)S(1)}) custom-call(bf16[1024,128]{1,0:T(8,128)(2,1)} %bitcast.31, bf16[1024,128]{1,0:T(8,128)(2,1)} %bitcast.26, bf16[1024,128]{1,0:T(8,128)(2,1)} %bitcast.28, bf16[1024,128]{1,0:T(8,128)(2,1)} %bitcast.33, ...), custom_call_target="tpu_custom_call" | custom-call | flops 1000 | bytes 1000 | tf_op jit(solution)/shard_map/heads/pallas_call | solution.py:27
  27.8 4.3 %collective-permute-start.4 = (bf16[64,2432]{1,0:T(8,128)(2,1)S(1)}, bf16[64,2432]{1,0:T(8,128)(2,1)S(1)}, u32[]{:S(2)}, u32[]{:S(2)}) collective-permute-start(bf16[64,2432]{1,0:T(8,128)(2,1)S(1)} %collective-permute-done.2.refs_0_), channel_id=1, source_target_pairs={{0,4},{1,29},{2,6},{3,31},{4,8},{5,1},{6,10},{7,3},{8,12},{9,5},{1... | collective-permute-start | bytes 933896 | tf_op jit(solution)/shard_map/ppermute | solution.py:201
  32.1 4.5 %collective-permute-start.3 = (f32[136,128]{1,0:T(8,128)S(1)}, f32[136,128]{1,0:T(8,128)S(1)}, u32[]{:S(2)}, u32[]{:S(2)}) collective-permute-start(f32[136,128]{1,0:T(8,128)S(1)} %multiply_add_fusion.5), channel_id=1, source_target_pairs={{64,0},{96,32},{128,64},{160,96},{192,128},{224,160},{256,192},{28... | collective-permute-start | bytes 208904 | tf_op jit(solution)/shard_map/ppermute | solution.py:210
  36.7 3.1 %collective-permute-start.9 = (bf16[64,2432]{1,0:T(8,128)(2,1)S(1)}, bf16[64,2432]{1,0:T(8,128)(2,1)S(1)}, u32[]{:S(2)}, u32[]{:S(2)}) collective-permute-start(bf16[64,2432]{1,0:T(8,128)(2,1)S(1)} %collective-permute-done.8.refs_1_), channel_id=1, source_target_pairs={{0,4},{1,29},{2,6},{3,31},{4,8},{5,1},{6,10},{7,3},{8,12},{9,5},{1... | collective-permute-start | bytes 933896 | tf_op jit(solution)/shard_map/ppermute | solution.py:201
  39.9 5.0 %collective-permute-start.6 = (bf16[64,2432]{1,0:T(8,128)(2,1)S(1)}, bf16[64,2432]{1,0:T(8,128)(2,1)}, u32[]{:S(2)}, u32[]{:S(2)}) collective-permute-start(bf16[64,2432]{1,0:T(8,128)(2,1)S(1)} %collective-permute-done.4.refs_2_), channel_id=1, source_target_pairs={{0,4},{1,29},{2,6},{3,31},{4,8},{5,1},{6,10},{7,3},{8,12},{9,5},{1... | collective-permute-start | bytes 933896 | tf_op jit(solution)/shard_map/ppermute | solution.py:201
  44.9 3.1 %collective-permute-done.9.refs_3_ = bf16[64,2432]{1,0:T(8,128)(2,1)S(1)} collective-permute-done((bf16[64,2432]{1,0:T(8,128)(2,1)S(1)}, bf16[64,2432]{1,0:T(8,128)(2,1)S(1)}, u32[]{:S(2)}, u32[]{:S(2)}) %collective-permute-start.9) | collective-permute-done | bytes 311328 | tf_op jit(solution)/shard_map/ppermute | solution.py:201
  48.0 6.5 %collective-permute-done.6.refs_0_ = bf16[64,2432]{1,0:T(8,128)(2,1)} collective-permute-done((bf16[64,2432]{1,0:T(8,128)(2,1)S(1)}, bf16[64,2432]{1,0:T(8,128)(2,1)}, u32[]{:S(2)}, u32[]{:S(2)}) %collective-permute-start.6) | collective-permute-done | bytes 311328 | tf_op jit(solution)/shard_map/ppermute | solution.py:201
  54.6 1.9 %collective-permute-start.10 = (bf16[256,2432]{1,0:T(8,128)(2,1)S(1)}, bf16[256,2432]{1,0:T(8,128)(2,1)S(1)}, u32[]{:S(2)}, u32[]{:S(2)}) collective-permute-start(bf16[256,2432]{1,0:T(8,128)(2,1)S(1)} %experts.5.refs_1_), channel_id=1, source_target_pairs={{0,1},{1,0},{2,3},{3,2},{4,5},{5,4},{6,7},{7,6},{8,9},{9,8},{10,11... | collective-permute-start | bytes 3735560 | tf_op jit(solution)/shard_map/experts/ppermute | solution.py:205
  56.5 2.1 %collective-permute-start.5 = (f32[136,128]{1,0:T(8,128)S(1)}, f32[136,128]{1,0:T(8,128)S(1)}, u32[]{:S(2)}, u32[]{:S(2)}) collective-permute-start(f32[136,128]{1,0:T(8,128)S(1)} %get-tuple-element.44), channel_id=1, source_target_pairs={{128,0},{160,32},{192,64},{224,96},{256,128},{288,160},{320,192},{... | collective-permute-start | bytes 208904 | tf_op jit(solution)/shard_map/ppermute | solution.py:210
  58.6 4.7 %collective-permute-start.11 = (bf16[64,2432]{1,0:T(8,128)(2,1)}, bf16[64,2432]{1,0:T(8,128)(2,1)S(1)}, u32[]{:S(2)}, u32[]{:S(2)}) collective-permute-start(bf16[64,2432]{1,0:T(8,128)(2,1)} %copy-done.5), channel_id=1, source_target_pairs={{0,4},{1,29},{2,6},{3,31},{4,8},{5,1},{6,10},{7,3},{8,12},{9,5},{1... | collective-permute-start | bytes 933896 | tf_op jit(solution)/shard_map/ppermute | solution.py:201
  63.4 2.4 %collective-permute-start.7 = (f32[136,128]{1,0:T(8,128)S(1)}, f32[136,128]{1,0:T(8,128)S(1)}, u32[]{:S(2)}, u32[]{:S(2)}) collective-permute-start(f32[136,128]{1,0:T(8,128)S(1)} %get-tuple-element.42), channel_id=1, source_target_pairs={{256,0},{288,32},{320,64},{352,96},{384,128},{416,160},{448,192},{... | collective-permute-start | bytes 208904 | tf_op jit(solution)/shard_map/ppermute | solution.py:210
  65.9 3.3 %collective-permute-start.12 = (bf16[64,2432]{1,0:T(8,128)(2,1)}, bf16[64,2432]{1,0:T(8,128)(2,1)S(1)}, u32[]{:S(2)}, u32[]{:S(2)}) collective-permute-start(bf16[64,2432]{1,0:T(8,128)(2,1)} %collective-permute-done.6.refs_0_), channel_id=1, source_target_pairs={{0,4},{1,29},{2,6},{3,31},{4,8},{5,1},{6,10},{7,3},{8,12},{9,5},{1... | collective-permute-start | bytes 933896 | tf_op jit(solution)/shard_map/ppermute | solution.py:201
  69.5 1.5 %copy-done = bf16[1,512,2304]{2,1,0:T(8,128)(2,1)S(1)} copy-done((bf16[1,512,2304]{2,1,0:T(8,128)(2,1)S(1)}, bf16[1,512,2304]{2,1,0:T(8,128)(2,1)}, u32[]{:S(2)}) %copy-start) | copy-done | bytes 2359320
  70.9 3.1 %experts.7.done_ref = bf16[288,512]{1,0:T(8,128)(2,1)S(1)} custom-call(s32[1]{0:T(128)} %bitcast.15.me_ref, bf16[576,2432]{1,0:T(8,128)(2,1)S(1)} %experts.6.rows_ref, bf16[512,2304]{1,0:T(8,128)(2,1)S(1)} %bitcast.24), custom_call_target="tpu_custom_call" | custom-call | flops 1000 | bytes 1000 | tf_op jit(solution)/shard_map/experts/pallas_call | solution.py:27
  74.1 3.9 %collective-permute-start.13 = (bf16[32,2432]{1,0:T(8,128)(2,1)S(1)}, bf16[32,2432]{1,0:T(8,128)(2,1)S(1)}, u32[]{:S(2)}, u32[]{:S(2)}) collective-permute-start(bf16[32,2432]{1,0:T(8,128)(2,1)S(1)} %slice.21), channel_id=1, source_target_pairs={{0,4},{1,29},{2,6},{3,31},{4,8},{5,1},{6,10},{7,3},{8,12},{9,5},{1... | collective-permute-start | bytes 466952 | tf_op jit(solution)/shard_map/ppermute | solution.py:201
  78.1 5.2 %collective-permute-done.13.refs_3_ = bf16[32,2432]{1,0:T(8,128)(2,1)S(1)} collective-permute-done((bf16[32,2432]{1,0:T(8,128)(2,1)S(1)}, bf16[32,2432]{1,0:T(8,128)(2,1)S(1)}, u32[]{:S(2)}, u32[]{:S(2)}) %collective-permute-start.13) | collective-permute-done | bytes 155680 | tf_op jit(solution)/shard_map/ppermute | solution.py:201
  84.4 6.8 %collective-permute-start.14 = (bf16[224,2432]{1,0:T(8,128)(2,1)S(1)}, bf16[224,2432]{1,0:T(8,128)(2,1)S(1)}, u32[]{:S(2)}, u32[]{:S(2)}) collective-permute-start(bf16[224,2432]{1,0:T(8,128)(2,1)S(1)} %experts.8.mine_ref), channel_id=1, source_target_pairs={{0,1},{1,0},{2,3},{3,2},{4,5},{5,4},{6,7},{7,6},{8,9},{9,8},{10,11... | collective-permute-start | bytes 3268616 | tf_op jit(solution)/shard_map/experts/ppermute | solution.py:205
  91.2 2.1 %arrival.1 = (bf16[1024,128]{1,0:T(8,128)(2,1)}, bf16[1024,128]{1,0:T(8,128)(2,1)}) custom-call(bf16[1024,128]{1,0:T(8,128)(2,1)} %bitcast.27, bf16[1024,128]{1,0:T(8,128)(2,1)} %bitcast.29, f32[136,128]{1,0:T(8,128)S(1)} %multiply_add_fusion.in_ref, f32[1024,128]{1,0:T(8,128)S(1)} %get-tuple-element.26.pk_ref, f32[1024,128]{1,0:T(8,128)S(1)} %copy-done.2, ...), custom_call_target="tpu_custom_call" | custom-call | flops 1000 | bytes 1000 | tf_op jit(solution)/shard_map/arrival/pallas_call | solution.py:27
  93.5 3.3 %experts.9 = bf16[32,16,512]{2,1,0:T(8,128)(2,1)} custom-call(s32[1]{0:T(128)} %bitcast.15.me_ref, bf16[288,512]{1,0:T(8,128)(2,1)S(1)} %experts.7.done_ref, bf16[224,2432]{1,0:T(8,128)(2,1)S(1)} %experts.8.mine_ref, bf16[224,2432]{1,0:T(8,128)(2,1)S(1)} %collective-permute-done.14.theirs_ref, bf16[512,2304]{1,0:T(8,128)(2,1)S(1)} %bitcast.25), custom_call_target="tpu_custom_call" | custom-call | flops 1000 | bytes 1000 | tf_op jit(solution)/shard_map/experts/pallas_call | solution.py:27
  (38 shorter events, 3.8 us)
Async XLA Ops:
  1.6 4.1 %collective-permute-start = (bf16[32,2432]{1,0:T(8,128)(2,1)S(1)}, bf16[32,2432]{1,0:T(8,128)(2,1)S(1)}, u32[]{:S(2)}, u32[]{:S(2)}) collective-permute-start(bf16[32,2432]{1,0:T(8,128)(2,1)S(1)} %pack.1.refs_0_), channel_id=1, source_target_pairs={{0,1},{1,0},{2,3},{3,2},{4,5},{5,4},{6,7},{7,6},{8,9},{9,8},{10,11... | collective-permute-start | bytes 466952 | tf_op jit(solution)/shard_map/ppermute | solution.py:205
  5.8 21.9 %collective-permute-start.2 = (bf16[64,2432]{1,0:T(8,128)(2,1)S(1)}, bf16[64,2432]{1,0:T(8,128)(2,1)S(1)}, u32[]{:S(2)}, u32[]{:S(2)}) collective-permute-start(bf16[64,2432]{1,0:T(8,128)(2,1)S(1)} %shard_map.129.refs_0_), channel_id=1, source_target_pairs={{0,2},{1,31},{2,4},{3,1},{4,6},{5,3},{6,8},{7,5},{8,10},{9,7},{10,... | collective-permute-start | bytes 933896 | tf_op jit(solution)/shard_map/ppermute | solution.py:201
  16.9 10.8 %collective-permute-start.1 = (f32[136,128]{1,0:T(8,128)S(1)}, f32[136,128]{1,0:T(8,128)S(1)}, u32[]{:S(2)}, u32[]{:S(2)}) collective-permute-start(f32[136,128]{1,0:T(8,128)S(1)} %message.1), channel_id=1, source_target_pairs={{32,0},{64,32},{96,64},{128,96},{160,128},{192,160},{224,192},{256... | collective-permute-start | bytes 208904 | tf_op jit(solution)/shard_map/ppermute | solution.py:210
  19.1 17.6 %collective-permute-start.8 = (bf16[64,2432]{1,0:T(8,128)(2,1)S(1)}, bf16[64,2432]{1,0:T(8,128)(2,1)S(1)}, u32[]{:S(2)}, u32[]{:S(2)}) collective-permute-start(bf16[64,2432]{1,0:T(8,128)(2,1)S(1)} %shard_map.129.refs_0_), channel_id=1, source_target_pairs={{0,4},{1,29},{2,6},{3,31},{4,8},{5,1},{6,10},{7,3},{8,12},{9,5},{1... | collective-permute-start | bytes 933896 | tf_op jit(solution)/shard_map/ppermute | solution.py:201
  26.9 0.8 copy-start.3
  27.7 20.3 %copy-start.1 = (f32[1024,128]{1,0:T(8,128)}, f32[1024,128]{1,0:T(8,128)S(1)}, u32[]{:S(2)}) copy-start(f32[1024,128]{1,0:T(8,128)S(1)} %get-tuple-element.31.pv_ref) | copy-start | bytes 1572868
  27.8 12.0 %collective-permute-start.4 = (bf16[64,2432]{1,0:T(8,128)(2,1)S(1)}, bf16[64,2432]{1,0:T(8,128)(2,1)S(1)}, u32[]{:S(2)}, u32[]{:S(2)}) collective-permute-start(bf16[64,2432]{1,0:T(8,128)(2,1)S(1)} %collective-permute-done.2.refs_0_), channel_id=1, source_target_pairs={{0,4},{1,29},{2,6},{3,31},{4,8},{5,1},{6,10},{7,3},{8,12},{9,5},{1... | collective-permute-start | bytes 933896 | tf_op jit(solution)/shard_map/ppermute | solution.py:201
  32.1 7.7 %collective-permute-start.3 = (f32[136,128]{1,0:T(8,128)S(1)}, f32[136,128]{1,0:T(8,128)S(1)}, u32[]{:S(2)}, u32[]{:S(2)}) collective-permute-start(f32[136,128]{1,0:T(8,128)S(1)} %multiply_add_fusion.5), channel_id=1, source_target_pairs={{64,0},{96,32},{128,64},{160,96},{192,128},{224,160},{256,192},{28... | collective-permute-start | bytes 208904 | tf_op jit(solution)/shard_map/ppermute | solution.py:210
  36.7 11.3 %collective-permute-start.9 = (bf16[64,2432]{1,0:T(8,128)(2,1)S(1)}, bf16[64,2432]{1,0:T(8,128)(2,1)S(1)}, u32[]{:S(2)}, u32[]{:S(2)}) collective-permute-start(bf16[64,2432]{1,0:T(8,128)(2,1)S(1)} %collective-permute-done.8.refs_1_), channel_id=1, source_target_pairs={{0,4},{1,29},{2,6},{3,31},{4,8},{5,1},{6,10},{7,3},{8,12},{9,5},{1... | collective-permute-start | bytes 933896 | tf_op jit(solution)/shard_map/ppermute | solution.py:201
  39.9 14.6 %collective-permute-start.6 = (bf16[64,2432]{1,0:T(8,128)(2,1)S(1)}, bf16[64,2432]{1,0:T(8,128)(2,1)}, u32[]{:S(2)}, u32[]{:S(2)}) collective-permute-start(bf16[64,2432]{1,0:T(8,128)(2,1)S(1)} %collective-permute-done.4.refs_2_), channel_id=1, source_target_pairs={{0,4},{1,29},{2,6},{3,31},{4,8},{5,1},{6,10},{7,3},{8,12},{9,5},{1... | collective-permute-start | bytes 933896 | tf_op jit(solution)/shard_map/ppermute | solution.py:201
  48.0 6.6 %copy-start.5 = (bf16[64,2432]{1,0:T(8,128)(2,1)}, bf16[64,2432]{1,0:T(8,128)(2,1)S(1)}, u32[]{:S(2)}) copy-start(bf16[64,2432]{1,0:T(8,128)(2,1)S(1)} %collective-permute-done.9.refs_3_) | copy-start | bytes 933892
  54.6 14.7 %collective-permute-start.10 = (bf16[256,2432]{1,0:T(8,128)(2,1)S(1)}, bf16[256,2432]{1,0:T(8,128)(2,1)S(1)}, u32[]{:S(2)}, u32[]{:S(2)}) collective-permute-start(bf16[256,2432]{1,0:T(8,128)(2,1)S(1)} %experts.5.refs_1_), channel_id=1, source_target_pairs={{0,1},{1,0},{2,3},{3,2},{4,5},{5,4},{6,7},{7,6},{8,9},{9,8},{10,11... | collective-permute-start | bytes 3735560 | tf_op jit(solution)/shard_map/experts/ppermute | solution.py:205
  56.5 6.8 %collective-permute-start.5 = (f32[136,128]{1,0:T(8,128)S(1)}, f32[136,128]{1,0:T(8,128)S(1)}, u32[]{:S(2)}, u32[]{:S(2)}) collective-permute-start(f32[136,128]{1,0:T(8,128)S(1)} %get-tuple-element.44), channel_id=1, source_target_pairs={{128,0},{160,32},{192,64},{224,96},{256,128},{288,160},{320,192},{... | collective-permute-start | bytes 208904 | tf_op jit(solution)/shard_map/ppermute | solution.py:210
  58.6 15.5 %collective-permute-start.11 = (bf16[64,2432]{1,0:T(8,128)(2,1)}, bf16[64,2432]{1,0:T(8,128)(2,1)S(1)}, u32[]{:S(2)}, u32[]{:S(2)}) collective-permute-start(bf16[64,2432]{1,0:T(8,128)(2,1)} %copy-done.5), channel_id=1, source_target_pairs={{0,4},{1,29},{2,6},{3,31},{4,8},{5,1},{6,10},{7,3},{8,12},{9,5},{1... | collective-permute-start | bytes 933896 | tf_op jit(solution)/shard_map/ppermute | solution.py:201
  63.4 14.6 %collective-permute-start.7 = (f32[136,128]{1,0:T(8,128)S(1)}, f32[136,128]{1,0:T(8,128)S(1)}, u32[]{:S(2)}, u32[]{:S(2)}) collective-permute-start(f32[136,128]{1,0:T(8,128)S(1)} %get-tuple-element.42), channel_id=1, source_target_pairs={{256,0},{288,32},{320,64},{352,96},{384,128},{416,160},{448,192},{... | collective-permute-start | bytes 208904 | tf_op jit(solution)/shard_map/ppermute | solution.py:210
  65.9 12.2 %collective-permute-start.12 = (bf16[64,2432]{1,0:T(8,128)(2,1)}, bf16[64,2432]{1,0:T(8,128)(2,1)S(1)}, u32[]{:S(2)}, u32[]{:S(2)}) collective-permute-start(bf16[64,2432]{1,0:T(8,128)(2,1)} %collective-permute-done.6.refs_0_), channel_id=1, source_target_pairs={{0,4},{1,29},{2,6},{3,31},{4,8},{5,1},{6,10},{7,3},{8,12},{9,5},{1... | collective-permute-start | bytes 933896 | tf_op jit(solution)/shard_map/ppermute | solution.py:201
  69.2 1.7 %copy-start = (bf16[1,512,2304]{2,1,0:T(8,128)(2,1)S(1)}, bf16[1,512,2304]{2,1,0:T(8,128)(2,1)}, u32[]{:S(2)}) copy-start(bf16[1,512,2304]{2,1,0:T(8,128)(2,1)} %param.19) | copy-start | bytes 7077892
  74.1 17.1 %copy-start.2 = (f32[1024,128]{1,0:T(8,128)S(1)}, f32[1024,128]{1,0:T(8,128)}, u32[]{:S(2)}) copy-start(f32[1024,128]{1,0:T(8,128)} %copy-done.1) | copy-start | bytes 1572868
  74.1 17.1 %copy-start.4 = (f32[1024,128]{1,0:T(8,128)S(1)}, f32[1024,128]{1,0:T(8,128)}, u32[]{:S(2)}) copy-start(f32[1024,128]{1,0:T(8,128)} %copy-done.3) | copy-start | bytes 1572868
  74.1 9.2 %collective-permute-start.13 = (bf16[32,2432]{1,0:T(8,128)(2,1)S(1)}, bf16[32,2432]{1,0:T(8,128)(2,1)S(1)}, u32[]{:S(2)}, u32[]{:S(2)}) collective-permute-start(bf16[32,2432]{1,0:T(8,128)(2,1)S(1)} %slice.21), channel_id=1, source_target_pairs={{0,4},{1,29},{2,6},{3,31},{4,8},{5,1},{6,10},{7,3},{8,12},{9,5},{1... | collective-permute-start | bytes 466952 | tf_op jit(solution)/shard_map/ppermute | solution.py:201
  84.4 9.2 %collective-permute-start.14 = (bf16[224,2432]{1,0:T(8,128)(2,1)S(1)}, bf16[224,2432]{1,0:T(8,128)(2,1)S(1)}, u32[]{:S(2)}, u32[]{:S(2)}) collective-permute-start(bf16[224,2432]{1,0:T(8,128)(2,1)S(1)} %experts.8.mine_ref), channel_id=1, source_target_pairs={{0,1},{1,0},{2,3},{3,2},{4,5},{5,4},{6,7},{7,6},{8,9},{9,8},{10,11... | collective-permute-start | bytes 3268616 | tf_op jit(solution)/shard_map/experts/ppermute | solution.py:205

commit v2 on v1

--- a/solution.py
+++ b/solution.py
@@ -106,7 +106,6 @@
         add_ref[n] = dot(grads, (queries * whole).astype(BF16), TN)
         state = state * jnp.exp(end) + dot(values, (keys * trail).astype(BF16), TN)
         tail_ref[part] = end - sums
-    later = jnp.zeros_like(ends[0])
     adjoint = jnp.zeros_like(state)
     for n in reversed(range(count)):
         part = pl.ds(n * CHUNK, CHUNK)
@@ -117,17 +116,23 @@
             pk_ref[part] += trail * dot(v_ref[part], arrived)
             scaled = (k_ref[part].astype(F32) * trail).astype(BF16)
             pv_ref[part] += dot(scaled, arrived, NT)
-        tail_ref[part] = jnp.exp(left + later)
-        later = later + ends[n]
         adjoint = add_ref[n] + jnp.exp(ends[n]) * adjoint
 
 
-def arrival_body(k_ref, v_ref, in_ref, pk_ref, pv_ref, tail_ref, kg_ref, vg_ref):
+def arrival_body(k_ref, v_ref, d_ref, in_ref, pk_ref, pv_ref, kg_ref, vg_ref):
     arrived = in_ref[: v_ref.shape[1]].astype(BF16)
-    tail = tail_ref[...]
-    kg_ref[...] = (pk_ref[...] + tail * dot(v_ref[...], arrived)).astype(BF16)
-    scaled = (k_ref[...].astype(F32) * tail).astype(BF16)
-    vg_ref[...] = (pv_ref[...] + dot(scaled, arrived, NT)).astype(BF16)
+    rows = lax.broadcasted_iota(jnp.int32, (CHUNK, CHUNK), 0)
+    columns = lax.broadcasted_iota(jnp.int32, (CHUNK, CHUNK), 1)
+    upper = (columns > rows).astype(BF16)
+    later = jnp.zeros((1, k_ref.shape[1]), F32)
+    for n in reversed(range(k_ref.shape[0] // CHUNK)):
+        part = pl.ds(n * CHUNK, CHUNK)
+        left = dot(upper, d_ref[part]) + later
+        later = left[:1] + d_ref[part][:1].astype(F32)
+        tail = jnp.exp(left)
+        kg_ref[part] = (pk_ref[part] + tail * dot(v_ref[part], arrived)).astype(BF16)
+        scaled = (k_ref[part].astype(F32) * tail).astype(BF16)
+        vg_ref[part] = (pv_ref[part] + dot(scaled, arrived, NT)).astype(BF16)
 
 
 def slots(expert, rows_ref, down_ref, store):
@@ -153,42 +158,48 @@
         low = jnp.where(hit, low, 0.0).astype(BF16)
         block = hidden[part]
         upper = block.astype(BF16)
-        lower = (block - upper.astype(F32)).astype(BF16)
-        result = dot(high, upper, TN) + dot(high, lower, TN) + dot(low, upper, TN)
+        result = dot(high, upper, TN) + dot(low, upper, TN)
         result = result.astype(BF16)
         for b in range(number):
             store(first + b, result[b * MOST : (b + 1) * MOST])
 
 
-def hidden_body(me_ref, rows_ref, down_ref, out_ref):
-    def store(block, result):
-        out_ref[block * MOST : (block + 1) * MOST] = result
-
-    slots(me_ref[0], rows_ref, down_ref, store)
-
-
-def sender(me, hops, other, sibling):
+def hidden_body(me_ref, *refs, first=0):
+    *parts, mine_ref, theirs_ref, own_ref, other_ref, rows_ref = refs
+    row = 0
+    for part in parts:
+        rows_ref[row : row + part.shape[0]] = part[...]
+        row += part.shape[0]
+    for turn, (down_ref, out_ref) in enumerate(((mine_ref, own_ref), (theirs_ref, other_ref))):
+
+        def store(block, result, out_ref=out_ref):
+            out_ref[first + block * MOST : first + (block + 1) * MOST] = result
+
+        slots(me_ref[0] ^ turn, rows_ref, down_ref, store)
+
+
+def last_body(me_ref, own_done, other_done, *refs):
+    *_, own_ref, other_ref, _ = refs
+    first = own_done.shape[0]
+    own_ref[:first] = own_done[...]
+    other_ref[:first] = other_done[...]
+    hidden_body(me_ref, *refs, first=first)
+
+
+BLOCKS = ((0, 0), *((hops, other) for hops in range(1, 8) for other in range(2)), (8, 0))
+
+
+def sender(me, block, sibling):
+    hops, other = block
     core = (me % 2 + sibling) % 2
     chip = (me // 2 + EXPERTS // 2 + (2 * core - 1) * hops) % (EXPERTS // 2)
     return chip * 2 + (core + other) % 2
 
 
-def last_body(me_ref, done_ref, mine_ref, theirs_ref, down_ref, out_ref, rows_ref):
-    me = me_ref[0]
-    here = [(hops, other, 0) for hops in range(1, 5) for other in (0, 1)]
-    blocks = [(0, 0, 0), (0, 1, 0), *here, *((h, o, 1) for h, o, _ in here)]
-    for i, block in enumerate(blocks):
-        out_ref[sender(me, *block)] = done_ref[i * MOST : (i + 1) * MOST]
-    here = [*((hops, other, 0) for hops in (5, 6, 7) for other in (0, 1)), (8, 0, 0)]
-    blocks = [*here, *((h, o, 1) for h, o, _ in here)]
-    half = mine_ref.shape[0]
-    rows_ref[:half] = mine_ref[...]
-    rows_ref[half:] = theirs_ref[...]
-
-    def store(i, result):
-        out_ref[sender(me, *blocks[i])] = result
-
-    slots(me, rows_ref, down_ref, store)
+def place_body(me_ref, mine_ref, theirs_ref, out_ref):
+    for sibling, ref in ((0, mine_ref), (1, theirs_ref)):
+        for i, block in enumerate(BLOCKS):
+            out_ref[sender(me_ref[0], block, sibling)] = ref[i * MOST : (i + 1) * MOST]
 
 
 def move(array, hops):
@@ -271,12 +282,17 @@
     me = lax.axis_index("exp").astype(jnp.int32).reshape(1)
     struct = jax.ShapeDtypeStruct
 
-    def hidden(array):
+    def hidden(body, *parts, done=()):
+        size = sum(part.shape[0] for part in parts)
+        slots_out = struct(
+            (size // ROWS * MOST + sum(part.shape[0] for part in done[:1]), hidden_width), BF16
+        )
         return call(
-            hidden_body,
-            struct((array.shape[0] // ROWS * MOST, hidden_width), BF16),
-            (me, array, down),
+            body,
+            (slots_out, slots_out),
+            (me, *done, *parts, down, down_theirs),
             smem=1,
+            scratch=(pltpu.VMEM((size, parts[0].shape[1]), BF16),),
         )
 
     with jax.named_scope("pack"):
@@ -297,24 +313,24 @@
         )
     theirs = after(swap(rows), message)
     both = join(rows, theirs)
+    down_theirs = swap(down)
     with jax.named_scope("heads"):
-        query_grad, key_part, value_part, tail = call(
+        query_grad, key_part, value_part = call(
             heads_body,
             (
                 struct((length, kd), BF16),
                 struct((length, kd), F32),
                 struct((length, vd), F32),
-                struct((length, kd), F32),
             ),
             (queries, keys, values, grads, decays, after(start, both)),
-            scratch=(pltpu.VMEM((length // CHUNK, vd, kd), F32),),
+            scratch=(pltpu.VMEM((length, kd), F32), pltpu.VMEM((length // CHUNK, vd, kd), F32)),
         )
 
     rows1, rows2 = move(both, 1), move(both, 2)
     incoming = after(from_later(after(message, both), 1), rows1)
     within = combine(message, incoming, vd)
-    rows3 = move(after(rows1, within, key_part), 2)
-    rows4 = move(rows2, 2)
+    rows3 = move(after(rows1, key_part), 2)
+    rows4 = move(after(rows2, within), 2)
     incoming = combine(incoming, after(from_later(within, 2), rows3), vd)
     within = combine(message, incoming, vd)
     rows5 = move(after(rows3, within), 2)
@@ -323,26 +339,25 @@
     within = combine(message, incoming, vd)
     rows7 = move(rows5, 2)
     with jax.named_scope("experts"):
-        early = join(rows1, rows2, rows3, after(rows4, rows5))
-        done = hidden(join(both, early, swap(early)))
-    rows8 = move(after(rows6, within, done)[:ROWS], 2)
-    incoming = combine(incoming, from_later(within, 8), vd)
+        done = hidden(hidden_body, rows, rows1, rows2, rows3, rows4, rows5, rows6)
+    rows8 = move(after(rows6, within)[:ROWS], 2)
+    incoming = combine(incoming, after(from_later(within, 8), *done), vd)
 
     with jax.named_scope("arrival"):
         key_grad, value_grad = call(
             arrival_body,
             (struct((length, kd), BF16), struct((length, vd), BF16)),
-            (keys, values, incoming, key_part, value_part, tail),
+            (keys, values, decays, incoming, key_part, value_part),
         )
 
     with jax.named_scope("experts"):
-        late = after(join(rows5, rows6, rows7, rows8), incoming)
+        last = after(rows8, incoming)
+        mine, theirs = hidden(last_body, rows7, last, done=done)
         hidden_grad = call(
-            last_body,
+            place_body,
             struct((EXPERTS, MOST, hidden_width), BF16),
-            (me, done, late, swap(late), down),
+            (me, mine, swap(theirs)),
             smem=1,
-            scratch=(pltpu.VMEM((2 * late.shape[0], late.shape[1]), BF16),),
         )
     return (
         query_grad.reshape(length, 1, kd),

time: 97.5 us -> 89.9 us (0.922)
  the two profiles are of different devices: /device:TPU:29 before, /device:TPU:41 now
where the time goes in v2:
time: 89.9 us; the launch traced here: 89.3 us
  starting transfers between devices  58.5 us (65%)
  Pallas kernels  20.7 us (23%)
  waiting for transfers between devices  7.37 us (8%)
  other arithmetic  0.99 us (1%)
  between operations  0.96 us (1%)
    ppermute x8, starting transfers between devices, move(): return lax.ppermute(array, 'exp', pairs)  36.4 us
    pallas_call x8, Pallas kernels, call(): pl.pallas_call(body, out_shape=outs, in_specs=[pl.BlockSpec(memory_space=...  20.7 us
    ppermute x3, starting transfers between devices, swap(): return lax.ppermute(array, 'exp', [(i, i ^ 1) for i in range(EXPERTS)])  12.1 us
    ppermute x4, starting transfers between devices, from_later(): return lax.ppermute(array, 'ctx', [(i + by, i) for i in range(peers - by)])  9.92 us
    ppermute x8, waiting for transfers between devices, move(): return lax.ppermute(array, 'exp', pairs)  6.66 us
  transfers between devices with their start and end apart: 15, of which 4 were waited for; matrix products, arithmetic and copies ran while one was open for 1% of the time, Pallas kernels for 18%

profile of v2, /device:TPU:41, one launch (start us, length us, event | category | flops | bytes accessed | tf_op | source)
XLA Modules:
  0.0 89.3 jit_solution(4388807654041204674)
XLA Ops:
  0.6 2.7 %collective-permute-start.11 = (bf16[512,2304]{1,0:T(8,128)(2,1)}, bf16[512,2304]{1,0:T(8,128)(2,1)}, u32[]{:S(2)}, u32[]{:S(2)}) collective-permute-start(bf16[512,2304]{1,0:T(8,128)(2,1)} %bitcast.24), channel_id=1, source_target_pairs={{0,1},{1,0},{2,3},{3,2},{4,5},{5,4},{6,7},{7,6},{8,9},{9,8},{10,11... | collective-permute-start | bytes 7077896 | tf_op jit(solution)/shard_map/ppermute | solution.py:216
  3.4 1.0 %pack.1.refs_0_ = bf16[32,2432]{1,0:T(8,128)(2,1)S(1)} custom-call(bf16[32,2304]{1,0:T(8,128)(2,1)} %rows_ref.1, f32[8,32]{1,0:T(8,128)} %bitcast.40, s32[8,32]{1,0:T(8,128)} %bitcast.41), custom_call_target="tpu_custom_call" | custom-call | flops 1000 | bytes 1000 | tf_op jit(solution)/shard_map/pack/pallas_call | solution.py:27
  4.4 1.9 %collective-permute-start = (bf16[32,2432]{1,0:T(8,128)(2,1)S(1)}, bf16[32,2432]{1,0:T(8,128)(2,1)S(1)}, u32[]{:S(2)}, u32[]{:S(2)}) collective-permute-start(bf16[32,2432]{1,0:T(8,128)(2,1)S(1)} %pack.1.refs_0_), channel_id=1, source_target_pairs={{0,1},{1,0},{2,3},{3,2},{4,5},{5,4},{6,7},{7,6},{8,9},{9,8},{10,11... | collective-permute-start | bytes 466952 | tf_op jit(solution)/shard_map/ppermute | solution.py:216
  6.3 1.5 %message.1 = f32[136,128]{1,0:T(8,128)S(1)} custom-call(bf16[1024,128]{1,0:T(8,128)(2,1)} %bitcast.30, bf16[1024,128]{1,0:T(8,128)(2,1)} %bitcast.32, bf16[1024,128]{1,0:T(8,128)(2,1)} %bitcast.27), custom_call_target="tpu_custom_call" | custom-call | flops 1000 | bytes 1000 | tf_op jit(solution)/shard_map/message/pallas_call | solution.py:27
  7.9 1.9 %collective-permute-start.2 = (bf16[64,2432]{1,0:T(8,128)(2,1)S(1)}, bf16[64,2432]{1,0:T(8,128)(2,1)S(1)}, u32[]{:S(2)}, u32[]{:S(2)}) collective-permute-start(bf16[64,2432]{1,0:T(8,128)(2,1)S(1)} %shard_map.129), channel_id=1, source_target_pairs={{0,2},{1,31},{2,4},{3,1},{4,6},{5,3},{6,8},{7,5},{8,10},{9,7},{10,... | collective-permute-start | bytes 933896 | tf_op jit(solution)/shard_map/ppermute | solution.py:212
  9.8 4.3 %collective-permute-start.1 = (f32[136,128]{1,0:T(8,128)S(1)}, f32[136,128]{1,0:T(8,128)S(1)}, u32[]{:S(2)}, u32[]{:S(2)}) collective-permute-start(f32[136,128]{1,0:T(8,128)S(1)} %message.1), channel_id=1, source_target_pairs={{32,0},{64,32},{96,64},{128,96},{160,128},{192,160},{224,192},{256... | collective-permute-start | bytes 208904 | tf_op jit(solution)/shard_map/ppermute | solution.py:221
  14.1 11.4 %collective-permute-start.8 = (bf16[64,2432]{1,0:T(8,128)(2,1)S(1)}, bf16[64,2432]{1,0:T(8,128)(2,1)}, u32[]{:S(2)}, u32[]{:S(2)}) collective-permute-start(bf16[64,2432]{1,0:T(8,128)(2,1)S(1)} %shard_map.129), channel_id=1, source_target_pairs={{0,4},{1,29},{2,6},{3,31},{4,8},{5,1},{6,10},{7,3},{8,12},{9,5},{1... | collective-permute-start | bytes 933896 | tf_op jit(solution)/shard_map/ppermute | solution.py:212
  25.5 4.7 %heads.1 = (bf16[1024,128]{1,0:T(8,128)(2,1)}, f32[1024,128]{1,0:T(8,128)S(1)}, f32[1024,128]{1,0:T(8,128)S(1)}) custom-call(bf16[1024,128]{1,0:T(8,128)(2,1)} %bitcast.31, bf16[1024,128]{1,0:T(8,128)(2,1)} %bitcast.34, bf16[1024,128]{1,0:T(8,128)(2,1)} %bitcast.36, bf16[1024,128]{1,0:T(8,128)(2,1)} %bitcast.33, bf16[1024,128]{1,0:T(8,128)(2,1)} %bitcast.28, ...), custom_call_target="tpu_custom_call" | custom-call | flops 1000 | bytes 1000 | tf_op jit(solution)/shard_map/heads/pallas_call | solution.py:27
  31.0 3.1 %collective-permute-start.4 = (bf16[64,2432]{1,0:T(8,128)(2,1)S(1)}, bf16[64,2432]{1,0:T(8,128)(2,1)}, u32[]{:S(2)}, u32[]{:S(2)}) collective-permute-start(bf16[64,2432]{1,0:T(8,128)(2,1)S(1)} %collective-permute-done.2.refs_1_), channel_id=1, source_target_pairs={{0,4},{1,29},{2,6},{3,31},{4,8},{5,1},{6,10},{7,3},{8,12},{9,5},{1... | collective-permute-start | bytes 933896 | tf_op jit(solution)/shard_map/ppermute | solution.py:212
  34.1 2.4 %collective-permute-start.3 = (f32[136,128]{1,0:T(8,128)S(1)}, f32[136,128]{1,0:T(8,128)S(1)}, u32[]{:S(2)}, u32[]{:S(2)}) collective-permute-start(f32[136,128]{1,0:T(8,128)S(1)} %multiply_add_fusion.5), channel_id=1, source_target_pairs={{64,0},{96,32},{128,64},{160,96},{192,128},{224,160},{256,192},{28... | collective-permute-start | bytes 208904 | tf_op jit(solution)/shard_map/ppermute | solution.py:221
  36.6 4.3 %collective-permute-start.9 = (bf16[64,2432]{1,0:T(8,128)(2,1)}, bf16[64,2432]{1,0:T(8,128)(2,1)}, u32[]{:S(2)}, u32[]{:S(2)}) collective-permute-start(bf16[64,2432]{1,0:T(8,128)(2,1)} %collective-permute-done.8.refs_2_), channel_id=1, source_target_pairs={{0,4},{1,29},{2,6},{3,31},{4,8},{5,1},{6,10},{7,3},{8,12},{9,5},{1... | collective-permute-start | bytes 933896 | tf_op jit(solution)/shard_map/ppermute | solution.py:212
  41.6 1.4 %collective-permute-done.4.refs_3_ = bf16[64,2432]{1,0:T(8,128)(2,1)} collective-permute-done((bf16[64,2432]{1,0:T(8,128)(2,1)S(1)}, bf16[64,2432]{1,0:T(8,128)(2,1)}, u32[]{:S(2)}, u32[]{:S(2)}) %collective-permute-start.4) | collective-permute-done | bytes 311328 | tf_op jit(solution)/shard_map/ppermute | solution.py:212
  43.7 4.4 %collective-permute-start.6 = (bf16[64,2432]{1,0:T(8,128)(2,1)}, bf16[64,2432]{1,0:T(8,128)(2,1)}, u32[]{:S(2)}, u32[]{:S(2)}) collective-permute-start(bf16[64,2432]{1,0:T(8,128)(2,1)} %collective-permute-done.4.refs_3_), channel_id=1, source_target_pairs={{0,4},{1,29},{2,6},{3,31},{4,8},{5,1},{6,10},{7,3},{8,12},{9,5},{1... | collective-permute-start | bytes 933896 | tf_op jit(solution)/shard_map/ppermute | solution.py:212
  48.1 1.9 %collective-permute-start.5 = (f32[136,128]{1,0:T(8,128)}, f32[136,128]{1,0:T(8,128)S(1)}, u32[]{:S(2)}, u32[]{:S(2)}) collective-permute-start(f32[136,128]{1,0:T(8,128)} %get-tuple-element.52), channel_id=1, source_target_pairs={{128,0},{160,32},{192,64},{224,96},{256,128},{288,160},{320,192},{... | collective-permute-start | bytes 208904 | tf_op jit(solution)/shard_map/ppermute | solution.py:221
  50.0 4.3 %collective-permute-start.10 = (bf16[64,2432]{1,0:T(8,128)(2,1)}, bf16[64,2432]{1,0:T(8,128)(2,1)S(1)}, u32[]{:S(2)}, u32[]{:S(2)}) collective-permute-start(bf16[64,2432]{1,0:T(8,128)(2,1)} %collective-permute-done.9.refs_4_), channel_id=1, source_target_pairs={{0,4},{1,29},{2,6},{3,31},{4,8},{5,1},{6,10},{7,3},{8,12},{9,5},{1... | collective-permute-start | bytes 933896 | tf_op jit(solution)/shard_map/ppermute | solution.py:212
  54.4 4.8 %collective-permute-done.6.refs_5_ = bf16[64,2432]{1,0:T(8,128)(2,1)} collective-permute-done((bf16[64,2432]{1,0:T(8,128)(2,1)}, bf16[64,2432]{1,0:T(8,128)(2,1)}, u32[]{:S(2)}, u32[]{:S(2)}) %collective-permute-start.6) | collective-permute-done | bytes 311328 | tf_op jit(solution)/shard_map/ppermute | solution.py:212
  59.3 1.3 %collective-permute-start.7 = (f32[136,128]{1,0:T(8,128)S(1)}, f32[136,128]{1,0:T(8,128)S(1)}, u32[]{:S(2)}, u32[]{:S(2)}) collective-permute-start(f32[136,128]{1,0:T(8,128)S(1)} %get-tuple-element.50), channel_id=1, source_target_pairs={{256,0},{288,32},{320,64},{352,96},{384,128},{416,160},{448,192},{... | collective-permute-start | bytes 208904 | tf_op jit(solution)/shard_map/ppermute | solution.py:221
  60.6 1.9 %collective-permute-start.12 = (bf16[64,2432]{1,0:T(8,128)(2,1)}, bf16[64,2432]{1,0:T(8,128)(2,1)S(1)}, u32[]{:S(2)}, u32[]{:S(2)}) collective-permute-start(bf16[64,2432]{1,0:T(8,128)(2,1)} %collective-permute-done.6.refs_5_), channel_id=1, source_target_pairs={{0,4},{1,29},{2,6},{3,31},{4,8},{5,1},{6,10},{7,3},{8,12},{9,5},{1... | collective-permute-start | bytes 933896 | tf_op jit(solution)/shard_map/ppermute | solution.py:212
  63.0 5.1 %collective-permute-start.13 = (bf16[32,2432]{1,0:T(8,128)(2,1)S(1)}, bf16[32,2432]{1,0:T(8,128)(2,1)S(1)}, u32[]{:S(2)}, u32[]{:S(2)}) collective-permute-start(bf16[32,2432]{1,0:T(8,128)(2,1)S(1)} %slice.21), channel_id=1, source_target_pairs={{0,4},{1,29},{2,6},{3,31},{4,8},{5,1},{6,10},{7,3},{8,12},{9,5},{1... | collective-permute-start | bytes 466952 | tf_op jit(solution)/shard_map/ppermute | solution.py:212
  68.1 6.4 %experts.3 = (bf16[208,512]{1,0:T(8,128)(2,1)S(1)}, bf16[208,512]{1,0:T(8,128)(2,1)S(1)}) custom-call(s32[1]{0:T(128)} %bitcast.13.me_ref, bf16[32,2432]{1,0:T(8,128)(2,1)S(1)} %pack.1.refs_0_, bf16[64,2432]{1,0:T(8,128)(2,1)S(1)} %collective-permute-done.2.refs_1_, bf16[64,2432]{1,0:T(8,128)(2,1)} %collective-permute-done.8.refs_2_, ...), custom_call_target="tpu_custom_call" | custom-call | flops 1000 | bytes 1000 | tf_op jit(solution)/shard_map/experts/pallas_call | solution.py:27
  74.7 3.8 %experts.4 = (bf16[256,512]{1,0:T(8,128)(2,1)S(1)}, bf16[256,512]{1,0:T(8,128)(2,1)S(1)}) custom-call(s32[1]{0:T(128)} %bitcast.13.me_ref, bf16[208,512]{1,0:T(8,128)(2,1)S(1)} %get-tuple-element.36.own_done, bf16[208,512]{1,0:T(8,128)(2,1)S(1)} %get-tuple-element.37.other_done, bf16[64,2432]{1,0:T(8,128)(2,1)S(1)} %collective-permute-done.12.refs_0_, ...), custom_call_target="tpu_custom_call" | custom-call | flops 1000 | bytes 1000 | tf_op jit(solution)/shard_map/experts/pallas_call | solution.py:27
  78.5 7.5 %collective-permute-start.14 = (bf16[256,512]{1,0:T(8,128)(2,1)S(1)}, bf16[256,512]{1,0:T(8,128)(2,1)S(1)}, u32[]{:S(2)}, u32[]{:S(2)}) collective-permute-start(bf16[256,512]{1,0:T(8,128)(2,1)S(1)} %get-tuple-element.45), channel_id=1, source_target_pairs={{0,1},{1,0},{2,3},{3,2},{4,5},{5,4},{6,7},{7,6},{8,9},{9,8},{10,11... | collective-permute-start | bytes 786440 | tf_op jit(solution)/shard_map/experts/ppermute | solution.py:216
  86.1 2.4 %arrival.1 = (bf16[1024,128]{1,0:T(8,128)(2,1)}, bf16[1024,128]{1,0:T(8,128)(2,1)}) custom-call(bf16[1024,128]{1,0:T(8,128)(2,1)} %bitcast.35, bf16[1024,128]{1,0:T(8,128)(2,1)} %bitcast.37, bf16[1024,128]{1,0:T(8,128)(2,1)} %bitcast.29, f32[136,128]{1,0:T(8,128)S(1)} %multiply_add_fusion.in_ref, f32[1024,128]{1,0:T(8,128)S(1)} %get-tuple-element.30.pk_ref, ...), custom_call_target="tpu_custom_call" | custom-call | flops 1000 | bytes 1000 | tf_op jit(solution)/shard_map/arrival/pallas_call | solution.py:27
  88.4 0.9 %experts.5 = bf16[32,16,512]{2,1,0:T(8,128)(2,1)} custom-call(s32[1]{0:T(128)} %bitcast.13.me_ref, bf16[256,512]{1,0:T(8,128)(2,1)S(1)} %get-tuple-element.44.mine_ref, bf16[256,512]{1,0:T(8,128)(2,1)S(1)} %collective-permute-done.14.theirs_ref), custom_call_target="tpu_custom_call" | custom-call | flops 1000 | bytes 1000 | tf_op jit(solution)/shard_map/experts/pallas_call | solution.py:27
  (30 shorter events, 3.0 us)
Async XLA Ops:
  0.6 67.5 %copy-start = (bf16[1,512,2304]{2,1,0:T(8,128)(2,1)S(1)}, bf16[1,512,2304]{2,1,0:T(8,128)(2,1)}, u32[]{:S(2)}) copy-start(bf16[1,512,2304]{2,1,0:T(8,128)(2,1)} %param.19) | copy-start | bytes 7077892
  0.6 67.5 %collective-permute-start.11 = (bf16[512,2304]{1,0:T(8,128)(2,1)}, bf16[512,2304]{1,0:T(8,128)(2,1)}, u32[]{:S(2)}, u32[]{:S(2)}) collective-permute-start(bf16[512,2304]{1,0:T(8,128)(2,1)} %bitcast.24), channel_id=1, source_target_pairs={{0,1},{1,0},{2,3},{3,2},{4,5},{5,4},{6,7},{7,6},{8,9},{9,8},{10,11... | collective-permute-start | bytes 7077896 | tf_op jit(solution)/shard_map/ppermute | solution.py:216
  4.4 3.5 %collective-permute-start = (bf16[32,2432]{1,0:T(8,128)(2,1)S(1)}, bf16[32,2432]{1,0:T(8,128)(2,1)S(1)}, u32[]{:S(2)}, u32[]{:S(2)}) collective-permute-start(bf16[32,2432]{1,0:T(8,128)(2,1)S(1)} %pack.1.refs_0_), channel_id=1, source_target_pairs={{0,1},{1,0},{2,3},{3,2},{4,5},{5,4},{6,7},{7,6},{8,9},{9,8},{10,11... | collective-permute-start | bytes 466952 | tf_op jit(solution)/shard_map/ppermute | solution.py:216
  7.9 23.1 %collective-permute-start.2 = (bf16[64,2432]{1,0:T(8,128)(2,1)S(1)}, bf16[64,2432]{1,0:T(8,128)(2,1)S(1)}, u32[]{:S(2)}, u32[]{:S(2)}) collective-permute-start(bf16[64,2432]{1,0:T(8,128)(2,1)S(1)} %shard_map.129), channel_id=1, source_target_pairs={{0,2},{1,31},{2,4},{3,1},{4,6},{5,3},{6,8},{7,5},{8,10},{9,7},{10,... | collective-permute-start | bytes 933896 | tf_op jit(solution)/shard_map/ppermute | solution.py:212
  9.8 21.2 %collective-permute-start.1 = (f32[136,128]{1,0:T(8,128)S(1)}, f32[136,128]{1,0:T(8,128)S(1)}, u32[]{:S(2)}, u32[]{:S(2)}) collective-permute-start(f32[136,128]{1,0:T(8,128)S(1)} %message.1), channel_id=1, source_target_pairs={{32,0},{64,32},{96,64},{128,96},{160,128},{192,160},{224,192},{256... | collective-permute-start | bytes 208904 | tf_op jit(solution)/shard_map/ppermute | solution.py:221
  14.1 22.5 %collective-permute-start.8 = (bf16[64,2432]{1,0:T(8,128)(2,1)S(1)}, bf16[64,2432]{1,0:T(8,128)(2,1)}, u32[]{:S(2)}, u32[]{:S(2)}) collective-permute-start(bf16[64,2432]{1,0:T(8,128)(2,1)S(1)} %shard_map.129), channel_id=1, source_target_pairs={{0,4},{1,29},{2,6},{3,31},{4,8},{5,1},{6,10},{7,3},{8,12},{9,5},{1... | collective-permute-start | bytes 933896 | tf_op jit(solution)/shard_map/ppermute | solution.py:212
  30.2 0.8 copy-start.1
  31.0 12.0 %collective-permute-start.4 = (bf16[64,2432]{1,0:T(8,128)(2,1)S(1)}, bf16[64,2432]{1,0:T(8,128)(2,1)}, u32[]{:S(2)}, u32[]{:S(2)}) collective-permute-start(bf16[64,2432]{1,0:T(8,128)(2,1)S(1)} %collective-permute-done.2.refs_1_), channel_id=1, source_target_pairs={{0,4},{1,29},{2,6},{3,31},{4,8},{5,1},{6,10},{7,3},{8,12},{9,5},{1... | collective-permute-start | bytes 933896 | tf_op jit(solution)/shard_map/ppermute | solution.py:212
  34.1 7.5 %collective-permute-start.3 = (f32[136,128]{1,0:T(8,128)S(1)}, f32[136,128]{1,0:T(8,128)S(1)}, u32[]{:S(2)}, u32[]{:S(2)}) collective-permute-start(f32[136,128]{1,0:T(8,128)S(1)} %multiply_add_fusion.5), channel_id=1, source_target_pairs={{64,0},{96,32},{128,64},{160,96},{192,128},{224,160},{256,192},{28... | collective-permute-start | bytes 208904 | tf_op jit(solution)/shard_map/ppermute | solution.py:221
  36.6 13.4 %collective-permute-start.9 = (bf16[64,2432]{1,0:T(8,128)(2,1)}, bf16[64,2432]{1,0:T(8,128)(2,1)}, u32[]{:S(2)}, u32[]{:S(2)}) collective-permute-start(bf16[64,2432]{1,0:T(8,128)(2,1)} %collective-permute-done.8.refs_2_), channel_id=1, source_target_pairs={{0,4},{1,29},{2,6},{3,31},{4,8},{5,1},{6,10},{7,3},{8,12},{9,5},{1... | collective-permute-start | bytes 933896 | tf_op jit(solution)/shard_map/ppermute | solution.py:212
  43.7 15.5 %collective-permute-start.6 = (bf16[64,2432]{1,0:T(8,128)(2,1)}, bf16[64,2432]{1,0:T(8,128)(2,1)}, u32[]{:S(2)}, u32[]{:S(2)}) collective-permute-start(bf16[64,2432]{1,0:T(8,128)(2,1)} %collective-permute-done.4.refs_3_), channel_id=1, source_target_pairs={{0,4},{1,29},{2,6},{3,31},{4,8},{5,1},{6,10},{7,3},{8,12},{9,5},{1... | collective-permute-start | bytes 933896 | tf_op jit(solution)/shard_map/ppermute | solution.py:212
  48.1 6.3 %collective-permute-start.5 = (f32[136,128]{1,0:T(8,128)}, f32[136,128]{1,0:T(8,128)S(1)}, u32[]{:S(2)}, u32[]{:S(2)}) collective-permute-start(f32[136,128]{1,0:T(8,128)} %get-tuple-element.52), channel_id=1, source_target_pairs={{128,0},{160,32},{192,64},{224,96},{256,128},{288,160},{320,192},{... | collective-permute-start | bytes 208904 | tf_op jit(solution)/shard_map/ppermute | solution.py:221
  50.0 12.9 %collective-permute-start.10 = (bf16[64,2432]{1,0:T(8,128)(2,1)}, bf16[64,2432]{1,0:T(8,128)(2,1)S(1)}, u32[]{:S(2)}, u32[]{:S(2)}) collective-permute-start(bf16[64,2432]{1,0:T(8,128)(2,1)} %collective-permute-done.9.refs_4_), channel_id=1, source_target_pairs={{0,4},{1,29},{2,6},{3,31},{4,8},{5,1},{6,10},{7,3},{8,12},{9,5},{1... | collective-permute-start | bytes 933896 | tf_op jit(solution)/shard_map/ppermute | solution.py:212
  59.3 15.3 %collective-permute-start.7 = (f32[136,128]{1,0:T(8,128)S(1)}, f32[136,128]{1,0:T(8,128)S(1)}, u32[]{:S(2)}, u32[]{:S(2)}) collective-permute-start(f32[136,128]{1,0:T(8,128)S(1)} %get-tuple-element.50), channel_id=1, source_target_pairs={{256,0},{288,32},{320,64},{352,96},{384,128},{416,160},{448,192},{... | collective-permute-start | bytes 208904 | tf_op jit(solution)/shard_map/ppermute | solution.py:221
  60.6 14.1 %collective-permute-start.12 = (bf16[64,2432]{1,0:T(8,128)(2,1)}, bf16[64,2432]{1,0:T(8,128)(2,1)S(1)}, u32[]{:S(2)}, u32[]{:S(2)}) collective-permute-start(bf16[64,2432]{1,0:T(8,128)(2,1)} %collective-permute-done.6.refs_5_), channel_id=1, source_target_pairs={{0,4},{1,29},{2,6},{3,31},{4,8},{5,1},{6,10},{7,3},{8,12},{9,5},{1... | collective-permute-start | bytes 933896 | tf_op jit(solution)/shard_map/ppermute | solution.py:212
  63.0 11.7 %collective-permute-start.13 = (bf16[32,2432]{1,0:T(8,128)(2,1)S(1)}, bf16[32,2432]{1,0:T(8,128)(2,1)S(1)}, u32[]{:S(2)}, u32[]{:S(2)}) collective-permute-start(bf16[32,2432]{1,0:T(8,128)(2,1)S(1)} %slice.21), channel_id=1, source_target_pairs={{0,4},{1,29},{2,6},{3,31},{4,8},{5,1},{6,10},{7,3},{8,12},{9,5},{1... | collective-permute-start | bytes 466952 | tf_op jit(solution)/shard_map/ppermute | solution.py:212
  74.7 11.4 %copy-start.2 = (f32[1024,128]{1,0:T(8,128)S(1)}, f32[1024,128]{1,0:T(8,128)}, u32[]{:S(2)}) copy-start(f32[1024,128]{1,0:T(8,128)} %copy-done.1) | copy-start | bytes 1572868
  78.5 9.9 %collective-permute-start.14 = (bf16[256,512]{1,0:T(8,128)(2,1)S(1)}, bf16[256,512]{1,0:T(8,128)(2,1)S(1)}, u32[]{:S(2)}, u32[]{:S(2)}) collective-permute-start(bf16[256,512]{1,0:T(8,128)(2,1)S(1)} %get-tuple-element.45), channel_id=1, source_target_pairs={{0,1},{1,0},{2,3},{3,2},{4,5},{5,4},{6,7},{7,6},{8,9},{9,8},{10,11... | collective-permute-start | bytes 786440 | tf_op jit(solution)/shard_map/experts/ppermute | solution.py:216

commit v3 on v2

--- a/solution.py
+++ b/solution.py
@@ -158,7 +158,7 @@
         low = jnp.where(hit, low, 0.0).astype(BF16)
         block = hidden[part]
         upper = block.astype(BF16)
-        result = dot(high, upper, TN) + dot(low, upper, TN)
+        result = dot(jnp.concatenate([high, low]), jnp.concatenate([upper, upper]), TN)
         result = result.astype(BF16)
         for b in range(number):
             store(first + b, result[b * MOST : (b + 1) * MOST])

time: 89.9 us -> 89.7 us (level)
  no operation moved by 1% of the time
where the time goes in v3:
time: 89.7 us; the launch traced here: 89 us
  starting transfers between devices  58.4 us (65%)
  Pallas kernels  20.4 us (23%)
  waiting for transfers between devices  7.37 us (8%)
  other arithmetic  0.99 us (1%)
  between operations  0.96 us (1%)
    ppermute x8, starting transfers between devices, move(): return lax.ppermute(array, 'exp', pairs)  36.4 us
    pallas_call x8, Pallas kernels, call(): pl.pallas_call(body, out_shape=outs, in_specs=[pl.BlockSpec(memory_space=...  20.4 us
    ppermute x3, starting transfers between devices, swap(): return lax.ppermute(array, 'exp', [(i, i ^ 1) for i in range(EXPERTS)])  12.1 us
    ppermute x4, starting transfers between devices, from_later(): return lax.ppermute(array, 'ctx', [(i + by, i) for i in range(peers - by)])  9.92 us
    ppermute x8, waiting for transfers between devices, move(): return lax.ppermute(array, 'exp', pairs)  6.66 us
  transfers between devices with their start and end apart: 15, of which 4 were waited for; matrix products, arithmetic and copies ran while one was open for 1% of the time, Pallas kernels for 18%

profile of v3, /device:TPU:41, one launch (start us, length us, event | category | flops | bytes accessed | tf_op | source)
XLA Modules:
  0.0 89.0 jit_solution(17552238638696505531)
XLA Ops:
  0.6 2.7 %collective-permute-start.11 = (bf16[512,2304]{1,0:T(8,128)(2,1)}, bf16[512,2304]{1,0:T(8,128)(2,1)}, u32[]{:S(2)}, u32[]{:S(2)}) collective-permute-start(bf16[512,2304]{1,0:T(8,128)(2,1)} %bitcast.24), channel_id=1, source_target_pairs={{0,1},{1,0},{2,3},{3,2},{4,5},{5,4},{6,7},{7,6},{8,9},{9,8},{10,11... | collective-permute-start | bytes 7077896 | tf_op jit(solution)/shard_map/ppermute | solution.py:216
  3.4 1.0 %pack.1.refs_0_ = bf16[32,2432]{1,0:T(8,128)(2,1)S(1)} custom-call(bf16[32,2304]{1,0:T(8,128)(2,1)} %rows_ref.1, f32[8,32]{1,0:T(8,128)} %bitcast.40, s32[8,32]{1,0:T(8,128)} %bitcast.41), custom_call_target="tpu_custom_call" | custom-call | flops 1000 | bytes 1000 | tf_op jit(solution)/shard_map/pack/pallas_call | solution.py:27
  4.4 1.9 %collective-permute-start = (bf16[32,2432]{1,0:T(8,128)(2,1)S(1)}, bf16[32,2432]{1,0:T(8,128)(2,1)S(1)}, u32[]{:S(2)}, u32[]{:S(2)}) collective-permute-start(bf16[32,2432]{1,0:T(8,128)(2,1)S(1)} %pack.1.refs_0_), channel_id=1, source_target_pairs={{0,1},{1,0},{2,3},{3,2},{4,5},{5,4},{6,7},{7,6},{8,9},{9,8},{10,11... | collective-permute-start | bytes 466952 | tf_op jit(solution)/shard_map/ppermute | solution.py:216
  6.3 1.5 %message.1 = f32[136,128]{1,0:T(8,128)S(1)} custom-call(bf16[1024,128]{1,0:T(8,128)(2,1)} %bitcast.30, bf16[1024,128]{1,0:T(8,128)(2,1)} %bitcast.32, bf16[1024,128]{1,0:T(8,128)(2,1)} %bitcast.27), custom_call_target="tpu_custom_call" | custom-call | flops 1000 | bytes 1000 | tf_op jit(solution)/shard_map/message/pallas_call | solution.py:27
  7.9 1.9 %collective-permute-start.2 = (bf16[64,2432]{1,0:T(8,128)(2,1)S(1)}, bf16[64,2432]{1,0:T(8,128)(2,1)S(1)}, u32[]{:S(2)}, u32[]{:S(2)}) collective-permute-start(bf16[64,2432]{1,0:T(8,128)(2,1)S(1)} %shard_map.129), channel_id=1, source_target_pairs={{0,2},{1,31},{2,4},{3,1},{4,6},{5,3},{6,8},{7,5},{8,10},{9,7},{10,... | collective-permute-start | bytes 933896 | tf_op jit(solution)/shard_map/ppermute | solution.py:212
  9.8 4.3 %collective-permute-start.1 = (f32[136,128]{1,0:T(8,128)S(1)}, f32[136,128]{1,0:T(8,128)S(1)}, u32[]{:S(2)}, u32[]{:S(2)}) collective-permute-start(f32[136,128]{1,0:T(8,128)S(1)} %message.1), channel_id=1, source_target_pairs={{32,0},{64,32},{96,64},{128,96},{160,128},{192,160},{224,192},{256... | collective-permute-start | bytes 208904 | tf_op jit(solution)/shard_map/ppermute | solution.py:221
  14.1 11.4 %collective-permute-start.8 = (bf16[64,2432]{1,0:T(8,128)(2,1)S(1)}, bf16[64,2432]{1,0:T(8,128)(2,1)}, u32[]{:S(2)}, u32[]{:S(2)}) collective-permute-start(bf16[64,2432]{1,0:T(8,128)(2,1)S(1)} %shard_map.129), channel_id=1, source_target_pairs={{0,4},{1,29},{2,6},{3,31},{4,8},{5,1},{6,10},{7,3},{8,12},{9,5},{1... | collective-permute-start | bytes 933896 | tf_op jit(solution)/shard_map/ppermute | solution.py:212
  25.5 4.7 %heads.1 = (bf16[1024,128]{1,0:T(8,128)(2,1)}, f32[1024,128]{1,0:T(8,128)S(1)}, f32[1024,128]{1,0:T(8,128)S(1)}) custom-call(bf16[1024,128]{1,0:T(8,128)(2,1)} %bitcast.31, bf16[1024,128]{1,0:T(8,128)(2,1)} %bitcast.34, bf16[1024,128]{1,0:T(8,128)(2,1)} %bitcast.36, bf16[1024,128]{1,0:T(8,128)(2,1)} %bitcast.33, bf16[1024,128]{1,0:T(8,128)(2,1)} %bitcast.28, ...), custom_call_target="tpu_custom_call" | custom-call | flops 1000 | bytes 1000 | tf_op jit(solution)/shard_map/heads/pallas_call | solution.py:27
  31.0 3.1 %collective-permute-start.4 = (bf16[64,2432]{1,0:T(8,128)(2,1)S(1)}, bf16[64,2432]{1,0:T(8,128)(2,1)}, u32[]{:S(2)}, u32[]{:S(2)}) collective-permute-start(bf16[64,2432]{1,0:T(8,128)(2,1)S(1)} %collective-permute-done.2.refs_1_), channel_id=1, source_target_pairs={{0,4},{1,29},{2,6},{3,31},{4,8},{5,1},{6,10},{7,3},{8,12},{9,5},{1... | collective-permute-start | bytes 933896 | tf_op jit(solution)/shard_map/ppermute | solution.py:212
  34.1 2.4 %collective-permute-start.3 = (f32[136,128]{1,0:T(8,128)S(1)}, f32[136,128]{1,0:T(8,128)S(1)}, u32[]{:S(2)}, u32[]{:S(2)}) collective-permute-start(f32[136,128]{1,0:T(8,128)S(1)} %multiply_add_fusion.5), channel_id=1, source_target_pairs={{64,0},{96,32},{128,64},{160,96},{192,128},{224,160},{256,192},{28... | collective-permute-start | bytes 208904 | tf_op jit(solution)/shard_map/ppermute | solution.py:221
  36.6 4.3 %collective-permute-start.9 = (bf16[64,2432]{1,0:T(8,128)(2,1)}, bf16[64,2432]{1,0:T(8,128)(2,1)}, u32[]{:S(2)}, u32[]{:S(2)}) collective-permute-start(bf16[64,2432]{1,0:T(8,128)(2,1)} %collective-permute-done.8.refs_2_), channel_id=1, source_target_pairs={{0,4},{1,29},{2,6},{3,31},{4,8},{5,1},{6,10},{7,3},{8,12},{9,5},{1... | collective-permute-start | bytes 933896 | tf_op jit(solution)/shard_map/ppermute | solution.py:212
  41.6 1.4 %collective-permute-done.4.refs_3_ = bf16[64,2432]{1,0:T(8,128)(2,1)} collective-permute-done((bf16[64,2432]{1,0:T(8,128)(2,1)S(1)}, bf16[64,2432]{1,0:T(8,128)(2,1)}, u32[]{:S(2)}, u32[]{:S(2)}) %collective-permute-start.4) | collective-permute-done | bytes 311328 | tf_op jit(solution)/shard_map/ppermute | solution.py:212
  43.7 4.4 %collective-permute-start.6 = (bf16[64,2432]{1,0:T(8,128)(2,1)}, bf16[64,2432]{1,0:T(8,128)(2,1)}, u32[]{:S(2)}, u32[]{:S(2)}) collective-permute-start(bf16[64,2432]{1,0:T(8,128)(2,1)} %collective-permute-done.4.refs_3_), channel_id=1, source_target_pairs={{0,4},{1,29},{2,6},{3,31},{4,8},{5,1},{6,10},{7,3},{8,12},{9,5},{1... | collective-permute-start | bytes 933896 | tf_op jit(solution)/shard_map/ppermute | solution.py:212
  48.1 1.9 %collective-permute-start.5 = (f32[136,128]{1,0:T(8,128)}, f32[136,128]{1,0:T(8,128)S(1)}, u32[]{:S(2)}, u32[]{:S(2)}) collective-permute-start(f32[136,128]{1,0:T(8,128)} %get-tuple-element.52), channel_id=1, source_target_pairs={{128,0},{160,32},{192,64},{224,96},{256,128},{288,160},{320,192},{... | collective-permute-start | bytes 208904 | tf_op jit(solution)/shard_map/ppermute | solution.py:221
  50.0 4.3 %collective-permute-start.10 = (bf16[64,2432]{1,0:T(8,128)(2,1)}, bf16[64,2432]{1,0:T(8,128)(2,1)S(1)}, u32[]{:S(2)}, u32[]{:S(2)}) collective-permute-start(bf16[64,2432]{1,0:T(8,128)(2,1)} %collective-permute-done.9.refs_4_), channel_id=1, source_target_pairs={{0,4},{1,29},{2,6},{3,31},{4,8},{5,1},{6,10},{7,3},{8,12},{9,5},{1... | collective-permute-start | bytes 933896 | tf_op jit(solution)/shard_map/ppermute | solution.py:212
  54.4 4.8 %collective-permute-done.6.refs_5_ = bf16[64,2432]{1,0:T(8,128)(2,1)} collective-permute-done((bf16[64,2432]{1,0:T(8,128)(2,1)}, bf16[64,2432]{1,0:T(8,128)(2,1)}, u32[]{:S(2)}, u32[]{:S(2)}) %collective-permute-start.6) | collective-permute-done | bytes 311328 | tf_op jit(solution)/shard_map/ppermute | solution.py:212
  59.3 1.3 %collective-permute-start.7 = (f32[136,128]{1,0:T(8,128)S(1)}, f32[136,128]{1,0:T(8,128)S(1)}, u32[]{:S(2)}, u32[]{:S(2)}) collective-permute-start(f32[136,128]{1,0:T(8,128)S(1)} %get-tuple-element.50), channel_id=1, source_target_pairs={{256,0},{288,32},{320,64},{352,96},{384,128},{416,160},{448,192},{... | collective-permute-start | bytes 208904 | tf_op jit(solution)/shard_map/ppermute | solution.py:221
  60.6 1.9 %collective-permute-start.12 = (bf16[64,2432]{1,0:T(8,128)(2,1)}, bf16[64,2432]{1,0:T(8,128)(2,1)S(1)}, u32[]{:S(2)}, u32[]{:S(2)}) collective-permute-start(bf16[64,2432]{1,0:T(8,128)(2,1)} %collective-permute-done.6.refs_5_), channel_id=1, source_target_pairs={{0,4},{1,29},{2,6},{3,31},{4,8},{5,1},{6,10},{7,3},{8,12},{9,5},{1... | collective-permute-start | bytes 933896 | tf_op jit(solution)/shard_map/ppermute | solution.py:212
  63.0 5.1 %collective-permute-start.13 = (bf16[32,2432]{1,0:T(8,128)(2,1)S(1)}, bf16[32,2432]{1,0:T(8,128)(2,1)S(1)}, u32[]{:S(2)}, u32[]{:S(2)}) collective-permute-start(bf16[32,2432]{1,0:T(8,128)(2,1)S(1)} %slice.21), channel_id=1, source_target_pairs={{0,4},{1,29},{2,6},{3,31},{4,8},{5,1},{6,10},{7,3},{8,12},{9,5},{1... | collective-permute-start | bytes 466952 | tf_op jit(solution)/shard_map/ppermute | solution.py:212
  68.1 6.2 %experts.3 = (bf16[208,512]{1,0:T(8,128)(2,1)S(1)}, bf16[208,512]{1,0:T(8,128)(2,1)S(1)}) custom-call(s32[1]{0:T(128)} %bitcast.13.me_ref, bf16[32,2432]{1,0:T(8,128)(2,1)S(1)} %pack.1.refs_0_, bf16[64,2432]{1,0:T(8,128)(2,1)S(1)} %collective-permute-done.2.refs_1_, bf16[64,2432]{1,0:T(8,128)(2,1)} %collective-permute-done.8.refs_2_, ...), custom_call_target="tpu_custom_call" | custom-call | flops 1000 | bytes 1000 | tf_op jit(solution)/shard_map/experts/pallas_call | solution.py:27
  74.5 3.7 %experts.4 = (bf16[256,512]{1,0:T(8,128)(2,1)S(1)}, bf16[256,512]{1,0:T(8,128)(2,1)S(1)}) custom-call(s32[1]{0:T(128)} %bitcast.13.me_ref, bf16[208,512]{1,0:T(8,128)(2,1)S(1)} %get-tuple-element.36.own_done, bf16[208,512]{1,0:T(8,128)(2,1)S(1)} %get-tuple-element.37.other_done, bf16[64,2432]{1,0:T(8,128)(2,1)S(1)} %collective-permute-done.12.refs_0_, ...), custom_call_target="tpu_custom_call" | custom-call | flops 1000 | bytes 1000 | tf_op jit(solution)/shard_map/experts/pallas_call | solution.py:27
  78.2 7.5 %collective-permute-start.14 = (bf16[256,512]{1,0:T(8,128)(2,1)S(1)}, bf16[256,512]{1,0:T(8,128)(2,1)S(1)}, u32[]{:S(2)}, u32[]{:S(2)}) collective-permute-start(bf16[256,512]{1,0:T(8,128)(2,1)S(1)} %get-tuple-element.45), channel_id=1, source_target_pairs={{0,1},{1,0},{2,3},{3,2},{4,5},{5,4},{6,7},{7,6},{8,9},{9,8},{10,11... | collective-permute-start | bytes 786440 | tf_op jit(solution)/shard_map/experts/ppermute | solution.py:216
  85.7 2.4 %arrival.1 = (bf16[1024,128]{1,0:T(8,128)(2,1)}, bf16[1024,128]{1,0:T(8,128)(2,1)}) custom-call(bf16[1024,128]{1,0:T(8,128)(2,1)} %bitcast.35, bf16[1024,128]{1,0:T(8,128)(2,1)} %bitcast.37, bf16[1024,128]{1,0:T(8,128)(2,1)} %bitcast.29, f32[136,128]{1,0:T(8,128)S(1)} %multiply_add_fusion.in_ref, f32[1024,128]{1,0:T(8,128)S(1)} %get-tuple-element.30.pk_ref, ...), custom_call_target="tpu_custom_call" | custom-call | flops 1000 | bytes 1000 | tf_op jit(solution)/shard_map/arrival/pallas_call | solution.py:27
  88.1 0.9 %experts.5 = bf16[32,16,512]{2,1,0:T(8,128)(2,1)} custom-call(s32[1]{0:T(128)} %bitcast.13.me_ref, bf16[256,512]{1,0:T(8,128)(2,1)S(1)} %get-tuple-element.44.mine_ref, bf16[256,512]{1,0:T(8,128)(2,1)S(1)} %collective-permute-done.14.theirs_ref), custom_call_target="tpu_custom_call" | custom-call | flops 1000 | bytes 1000 | tf_op jit(solution)/shard_map/experts/pallas_call | solution.py:27
  (30 shorter events, 3.0 us)
Async XLA Ops:
  0.6 67.5 %copy-start = (bf16[1,512,2304]{2,1,0:T(8,128)(2,1)S(1)}, bf16[1,512,2304]{2,1,0:T(8,128)(2,1)}, u32[]{:S(2)}) copy-start(bf16[1,512,2304]{2,1,0:T(8,128)(2,1)} %param.19) | copy-start | bytes 7077892
  0.6 67.5 %collective-permute-start.11 = (bf16[512,2304]{1,0:T(8,128)(2,1)}, bf16[512,2304]{1,0:T(8,128)(2,1)}, u32[]{:S(2)}, u32[]{:S(2)}) collective-permute-start(bf16[512,2304]{1,0:T(8,128)(2,1)} %bitcast.24), channel_id=1, source_target_pairs={{0,1},{1,0},{2,3},{3,2},{4,5},{5,4},{6,7},{7,6},{8,9},{9,8},{10,11... | collective-permute-start | bytes 7077896 | tf_op jit(solution)/shard_map/ppermute | solution.py:216
  4.4 3.5 %collective-permute-start = (bf16[32,2432]{1,0:T(8,128)(2,1)S(1)}, bf16[32,2432]{1,0:T(8,128)(2,1)S(1)}, u32[]{:S(2)}, u32[]{:S(2)}) collective-permute-start(bf16[32,2432]{1,0:T(8,128)(2,1)S(1)} %pack.1.refs_0_), channel_id=1, source_target_pairs={{0,1},{1,0},{2,3},{3,2},{4,5},{5,4},{6,7},{7,6},{8,9},{9,8},{10,11... | collective-permute-start | bytes 466952 | tf_op jit(solution)/shard_map/ppermute | solution.py:216
  7.9 23.1 %collective-permute-start.2 = (bf16[64,2432]{1,0:T(8,128)(2,1)S(1)}, bf16[64,2432]{1,0:T(8,128)(2,1)S(1)}, u32[]{:S(2)}, u32[]{:S(2)}) collective-permute-start(bf16[64,2432]{1,0:T(8,128)(2,1)S(1)} %shard_map.129), channel_id=1, source_target_pairs={{0,2},{1,31},{2,4},{3,1},{4,6},{5,3},{6,8},{7,5},{8,10},{9,7},{10,... | collective-permute-start | bytes 933896 | tf_op jit(solution)/shard_map/ppermute | solution.py:212
  9.8 21.2 %collective-permute-start.1 = (f32[136,128]{1,0:T(8,128)S(1)}, f32[136,128]{1,0:T(8,128)S(1)}, u32[]{:S(2)}, u32[]{:S(2)}) collective-permute-start(f32[136,128]{1,0:T(8,128)S(1)} %message.1), channel_id=1, source_target_pairs={{32,0},{64,32},{96,64},{128,96},{160,128},{192,160},{224,192},{256... | collective-permute-start | bytes 208904 | tf_op jit(solution)/shard_map/ppermute | solution.py:221
  14.1 22.5 %collective-permute-start.8 = (bf16[64,2432]{1,0:T(8,128)(2,1)S(1)}, bf16[64,2432]{1,0:T(8,128)(2,1)}, u32[]{:S(2)}, u32[]{:S(2)}) collective-permute-start(bf16[64,2432]{1,0:T(8,128)(2,1)S(1)} %shard_map.129), channel_id=1, source_target_pairs={{0,4},{1,29},{2,6},{3,31},{4,8},{5,1},{6,10},{7,3},{8,12},{9,5},{1... | collective-permute-start | bytes 933896 | tf_op jit(solution)/shard_map/ppermute | solution.py:212
  30.2 0.8 copy-start.1
  31.0 12.0 %collective-permute-start.4 = (bf16[64,2432]{1,0:T(8,128)(2,1)S(1)}, bf16[64,2432]{1,0:T(8,128)(2,1)}, u32[]{:S(2)}, u32[]{:S(2)}) collective-permute-start(bf16[64,2432]{1,0:T(8,128)(2,1)S(1)} %collective-permute-done.2.refs_1_), channel_id=1, source_target_pairs={{0,4},{1,29},{2,6},{3,31},{4,8},{5,1},{6,10},{7,3},{8,12},{9,5},{1... | collective-permute-start | bytes 933896 | tf_op jit(solution)/shard_map/ppermute | solution.py:212
  34.1 7.5 %collective-permute-start.3 = (f32[136,128]{1,0:T(8,128)S(1)}, f32[136,128]{1,0:T(8,128)S(1)}, u32[]{:S(2)}, u32[]{:S(2)}) collective-permute-start(f32[136,128]{1,0:T(8,128)S(1)} %multiply_add_fusion.5), channel_id=1, source_target_pairs={{64,0},{96,32},{128,64},{160,96},{192,128},{224,160},{256,192},{28... | collective-permute-start | bytes 208904 | tf_op jit(solution)/shard_map/ppermute | solution.py:221
  36.6 13.4 %collective-permute-start.9 = (bf16[64,2432]{1,0:T(8,128)(2,1)}, bf16[64,2432]{1,0:T(8,128)(2,1)}, u32[]{:S(2)}, u32[]{:S(2)}) collective-permute-start(bf16[64,2432]{1,0:T(8,128)(2,1)} %collective-permute-done.8.refs_2_), channel_id=1, source_target_pairs={{0,4},{1,29},{2,6},{3,31},{4,8},{5,1},{6,10},{7,3},{8,12},{9,5},{1... | collective-permute-start | bytes 933896 | tf_op jit(solution)/shard_map/ppermute | solution.py:212
  43.7 15.5 %collective-permute-start.6 = (bf16[64,2432]{1,0:T(8,128)(2,1)}, bf16[64,2432]{1,0:T(8,128)(2,1)}, u32[]{:S(2)}, u32[]{:S(2)}) collective-permute-start(bf16[64,2432]{1,0:T(8,128)(2,1)} %collective-permute-done.4.refs_3_), channel_id=1, source_target_pairs={{0,4},{1,29},{2,6},{3,31},{4,8},{5,1},{6,10},{7,3},{8,12},{9,5},{1... | collective-permute-start | bytes 933896 | tf_op jit(solution)/shard_map/ppermute | solution.py:212
  48.1 6.3 %collective-permute-start.5 = (f32[136,128]{1,0:T(8,128)}, f32[136,128]{1,0:T(8,128)S(1)}, u32[]{:S(2)}, u32[]{:S(2)}) collective-permute-start(f32[136,128]{1,0:T(8,128)} %get-tuple-element.52), channel_id=1, source_target_pairs={{128,0},{160,32},{192,64},{224,96},{256,128},{288,160},{320,192},{... | collective-permute-start | bytes 208904 | tf_op jit(solution)/shard_map/ppermute | solution.py:221
  50.0 12.9 %collective-permute-start.10 = (bf16[64,2432]{1,0:T(8,128)(2,1)}, bf16[64,2432]{1,0:T(8,128)(2,1)S(1)}, u32[]{:S(2)}, u32[]{:S(2)}) collective-permute-start(bf16[64,2432]{1,0:T(8,128)(2,1)} %collective-permute-done.9.refs_4_), channel_id=1, source_target_pairs={{0,4},{1,29},{2,6},{3,31},{4,8},{5,1},{6,10},{7,3},{8,12},{9,5},{1... | collective-permute-start | bytes 933896 | tf_op jit(solution)/shard_map/ppermute | solution.py:212
  59.3 15.0 %collective-permute-start.7 = (f32[136,128]{1,0:T(8,128)S(1)}, f32[136,128]{1,0:T(8,128)S(1)}, u32[]{:S(2)}, u32[]{:S(2)}) collective-permute-start(f32[136,128]{1,0:T(8,128)S(1)} %get-tuple-element.50), channel_id=1, source_target_pairs={{256,0},{288,32},{320,64},{352,96},{384,128},{416,160},{448,192},{... | collective-permute-start | bytes 208904 | tf_op jit(solution)/shard_map/ppermute | solution.py:221
  60.6 13.8 %collective-permute-start.12 = (bf16[64,2432]{1,0:T(8,128)(2,1)}, bf16[64,2432]{1,0:T(8,128)(2,1)S(1)}, u32[]{:S(2)}, u32[]{:S(2)}) collective-permute-start(bf16[64,2432]{1,0:T(8,128)(2,1)} %collective-permute-done.6.refs_5_), channel_id=1, source_target_pairs={{0,4},{1,29},{2,6},{3,31},{4,8},{5,1},{6,10},{7,3},{8,12},{9,5},{1... | collective-permute-start | bytes 933896 | tf_op jit(solution)/shard_map/ppermute | solution.py:212
  63.0 11.5 %collective-permute-start.13 = (bf16[32,2432]{1,0:T(8,128)(2,1)S(1)}, bf16[32,2432]{1,0:T(8,128)(2,1)S(1)}, u32[]{:S(2)}, u32[]{:S(2)}) collective-permute-start(bf16[32,2432]{1,0:T(8,128)(2,1)S(1)} %slice.21), channel_id=1, source_target_pairs={{0,4},{1,29},{2,6},{3,31},{4,8},{5,1},{6,10},{7,3},{8,12},{9,5},{1... | collective-permute-start | bytes 466952 | tf_op jit(solution)/shard_map/ppermute | solution.py:212
  74.4 11.3 %copy-start.2 = (f32[1024,128]{1,0:T(8,128)S(1)}, f32[1024,128]{1,0:T(8,128)}, u32[]{:S(2)}) copy-start(f32[1024,128]{1,0:T(8,128)} %copy-done.1) | copy-start | bytes 1572868
  78.2 9.9 %collective-permute-start.14 = (bf16[256,512]{1,0:T(8,128)(2,1)S(1)}, bf16[256,512]{1,0:T(8,128)(2,1)S(1)}, u32[]{:S(2)}, u32[]{:S(2)}) collective-permute-start(bf16[256,512]{1,0:T(8,128)(2,1)S(1)} %get-tuple-element.45), channel_id=1, source_target_pairs={{0,1},{1,0},{2,3},{3,2},{4,5},{5,4},{6,7},{7,6},{8,9},{9,8},{10,11... | collective-permute-start | bytes 786440 | tf_op jit(solution)/shard_map/experts/ppermute | solution.py:216
